TPU v7x, 512 devices: a whole 4x8x8 slice. The times are simulated.
512 devices in a mesh: member: 8 (over z_lo, core), grid: 64 (over x, y, z_hi).
Axes of the slice: x: 4, y: 8, z: 8 (z_hi: 2, z_lo: 4; z = z_hi * 4 + z_lo), core: 2. Of those that a mesh axis runs over, the one named last changes fastest.
Arguments:
- latent: bfloat16 [8, 1024, 32768], P('member', None, 'grid'), may hold values from -6 to 6
- w_in: bfloat16 [1024, 512], replicated, may hold values from -0.1875 to 0.1875
- b_in: float32 [512], replicated, may hold values from -3 to 3
- output_weight: bfloat16 [512, 83], replicated, may hold values from -0.25 to 0.25
- output_bias: float32 [83], replicated, may hold values from -3 to 3
- observed_field: float32 [83, 32768], P(None, 'grid'), may hold values from -6 to 6
- area: float32 [32768], P('grid'), may hold values from 0.2 to 2
Outputs:
- loss: float32 [32768], P('grid')
- grad_w_in: bfloat16 [1024, 512], replicated
- grad_b_in: float32 [512], replicated
- grad_w_out: float32 [512, 83], replicated
- grad_b_out: float32 [83], replicated
All inputs are finite; a program needn't handle non-finite values.
Results may differ from a plain program's by a relative error of at most 0.006.
Values may be sent and summed in bfloat16 or wider, within the bound.
A program may use at most 64 MiB of HBM per device.

v0:
```python
import math

import jax
import jax.numpy as jnp
from jax import lax
from jax.sharding import PartitionSpec as P

EPSILON = 1e-05


def activation(values):
    return jax.nn.gelu(values, approximate=True)


def euclid_norm(run_difference):
    return jnp.sqrt(jnp.mean(run_difference * run_difference, axis=-2) + EPSILON)


def per_device(latent, w_in, b_in, output_weight, output_bias, observed_field, area):
    latent_cols = latent[0]
    run_total = lax.axis_size("member")
    columns = latent_cols.shape[1] * lax.axis_size("grid")
    quantity_number = observed_field.shape[0]
    pre_act = jnp.dot(w_in.T, latent_cols, preferred_element_type=jnp.float32) + b_in[:, None]
    hidden_full, gelu_back = jax.vjp(activation, pre_act)
    hidden_units = hidden_full.astype(jnp.bfloat16)
    lone_run_field = (
        jnp.dot(output_weight.T, hidden_units, preferred_element_type=jnp.float32)
        + output_bias[:, None]
    ).astype(jnp.bfloat16)
    current_run_field = lone_run_field.astype(jnp.float32)
    observation_norm = euclid_norm(current_run_field - observed_field)
    run_difference = current_run_field[None] - lax.all_gather(
        lone_run_field[None], "member", axis=0, tiled=True
    ).astype(jnp.float32)
    pair_len = euclid_norm(run_difference)
    couple_derivative = jnp.sum(run_difference / (quantity_number * pair_len[:, None, :]), axis=0)
    pair_dist = jnp.sum(pair_len, axis=0)
    share = observation_norm / run_total - pair_dist / (2.0 * run_total * run_total)
    loss = lax.psum(share, "member")
    coupling_factor = area * (quantity_number * math.sqrt(run_total / columns))
    derivative_wrt_run = coupling_factor * (
        (current_run_field - observed_field) / (quantity_number * observation_norm) / run_total
        - couple_derivative / (run_total * run_total)
    )
    grad_low = derivative_wrt_run.astype(jnp.bfloat16)
    part_w_out = jnp.dot(hidden_units, grad_low.T, preferred_element_type=jnp.float32)
    part_b_out = jnp.sum(derivative_wrt_run, axis=1)
    grad_hidden = jnp.dot(output_weight, grad_low, preferred_element_type=jnp.float32)
    grad_pre = gelu_back(grad_hidden)[0]
    part_b_in = jnp.sum(grad_pre, axis=1)
    part_w_in = jnp.dot(
        latent_cols, grad_pre.astype(jnp.bfloat16).T, preferred_element_type=jnp.float32
    )
    grad_w_in, grad_b_in, grad_w_out, grad_b_out = lax.psum(
        (part_w_in, part_b_in, part_w_out, part_b_out), ("member", "grid")
    )
    result_w_in = grad_w_in.astype(jnp.bfloat16)
    return (loss, result_w_in, grad_b_in, grad_w_out, grad_b_out)


def solution(mesh):
    placed = (P("member", None, "grid"), P(), P(), P(), P(), P(None, "grid"), P("grid"))
    return jax.shard_map(
        per_device,
        mesh=mesh,
        in_specs=placed,
        out_specs=(P("grid"), P(), P(), P(), P()),
        check_vma=False,
    )
```

profile of v0, /device:TPU:1, one launch (start us, length us, event | category | flops | bytes accessed | tf_op | source)
XLA Modules:
  0.0 306.2 jit_solution(1979263933458094572)
XLA Ops:
  7.2 0.0 copy-start
  7.2 0.0 all-reduce.4.cloned.1.call-start
  7.2 0.8 broadcast_multiply_fusion
  8.0 0.4 copy-done
  8.4 0.0 copy-start.1
  8.4 0.0 copy-start.2
  8.4 2.3 multiply_convert_fusion
  10.7 0.0 copy-done.1
  10.7 0.0 copy-done.2
  10.7 0.0 copy-done.3
  10.7 0.3 multiply_reduce_fusion
  11.1 22.3 %all-gather.1 = bf16[8,83,512]{2,1,0:T(8,128)(2,1)S(1)} all-gather(bf16[1,83,512]{2,1,0:T(8,128)(2,1)S(1)} %bitcast.32), channel_id=2, replica_groups=mesh['member'=8,'grid'=64] {'member'}, dimensions={0}, use_global_device_ids=true | all-gather | bytes 764928 | tf_op jit(solution)/shard_map/all_gather | solution.py:33
  33.4 0.2 fusion.2
  33.6 0.2 fusion.3
  33.8 0.2 fusion.21
  34.0 0.9 fusion.15
  34.9 0.0 all-reduce.4.cloned.1.call-update
  34.9 0.9 fusion.22
  35.8 0.8 convolution_bitcast_fusion
  36.6 110.6 %all-reduce.5 = (bf16[1024,512]{0,1:T(8,128)(2,1)}, f32[512]{0:T(512)}, f32[83]{0:T(128)}) all-reduce(f32[1024,512]{0,1:T(8,128)S(1)} %convolution_bitcast_fusion, f32[512]{0:T(512)S(1)} %get-tuple-element.28, f32[83]{0:T(128)S(1)} %get-tuple-element.18), channel_id=1, replica_groups=mesh['member'=8,'grid'=64] {'member','grid'}, use_global_device_ids=true, to_apply=%region_5.0 | all-reduce | flops 524883 | bytes 3150488 | tf_op jit(solution)/shard_map/psum | solution.py:55
  147.2 2.3 copy.13
  149.5 14.2 %psum.35 = f32[512]{0:T(512)} all-reduce(f32[512]{0:T(512)S(1)} %get-tuple-element.23), channel_id=1, replica_groups=mesh['member'=8,'grid'=64] {'member'}, use_global_device_ids=true, to_apply=%region_3.0 | all-reduce | flops 512 | bytes 4096 | tf_op jit(solution)/shard_map/psum | solution.py:40
  163.7 134.1 %all-reduce.4.cloned.1.call-done = f32[512,83]{0,1:T(8,128)} async-done(((f32[512,83]{0,1:T(8,128)}), f32[512,83]{0,1:T(8,128)}) %all-reduce.4.cloned.1.call-update) | async-done | bytes 170000 | tf_op jit(solution)/shard_map/psum | solution.py:55
  297.8 1.6 copy.19
  (4 shorter events, 0.1 us)
Async XLA Ops:
  7.2 1.2 copy-start
  7.2 290.6 %all-reduce.4.cloned.1.call-start = ((), (), s32[]{:S(2)}) async-start(), calls=%async_computation | async-start | bytes 360448 | tf_op jit(solution)/shard_map/psum | solution.py:55
  8.4 2.3 copy-start.1
  8.4 2.3 copy-start.2
  8.4 2.3 copy-start.3
Sparse Core Ops, SparseCore 0:
  35.0 262.7 all-reduce.3
where the time goes:
time: 306 us
  blocking collectives  147 us (48%)
  waiting for transfers between devices  134 us (44%)
  between operations  14.1 us (5%)
  matrix products  5.11 us (2%)
  local copies, waits for them, and re-layouts  4.32 us (1%)
    psum x1, waiting for transfers between devices, per_device(): lax.psum((part_w_in, part_b_in, part_w_out, part_b_out), ('member', 'grid'))  134 us
    psum x1, blocking collectives, per_device(): lax.psum((part_w_in, part_b_in, part_w_out, part_b_out), ('member', 'grid'))  111 us
    all_gather x1, blocking collectives, per_device(): lax.all_gather(lone_run_field[None], 'member', axis=0, tiled=True)  22.3 us
    psum x1, blocking collectives, per_device(): loss = lax.psum(share, 'member')  14.2 us
  transfers between devices with their start and end apart: 1, of which 1 were waited for; matrix products, arithmetic and copies ran while one was open for 1% of the time, Pallas kernels for 0%

commit v1 on v0

v1 whole, which is shorter than its diff:
```python
import math

import jax
import jax.numpy as jnp
from jax import lax
from jax.experimental import pallas as pl
from jax.experimental.pallas import tpu as pltpu
from jax.sharding import PartitionSpec as P

MESH = pl.DeviceIdType.MESH
F32 = jnp.float32
BF16 = jnp.bfloat16
EPSILON = 1e-05
GELU_A = math.sqrt(2.0 / math.pi)
GELU_B = 0.044715

DIN, HID, VARS = 1024, 512, 83
COLS = 512
FOLD = 48
NX, NU = 4, 8
FAR4 = (2, 1, 3)
FAR8 = (4, 3, 5, 2, 6, 1, 7)
N_SEMS = 160


def dot(a, b):
    return jnp.dot(a, b, preferred_element_type=F32)


def dot_nt(a, b):
    return lax.dot_general(a, b, (((1,), (1,)), ((), ())), preferred_element_type=F32)


def kernel(
    total_columns,
    lat_hbm, win_hbm, bin_ref, wo_ref, bo_ref, obs_ref, area_ref,
    loss_ref, gw_ref, small_ref, gwo_ref,
    lat, win, win_t, bias, pre, dgelu, hidden, wop, wop_t, row, obs_pad,
    f_send, f_recv, g_send, g_recv, loss_recv, gl, gp,
    sib_send, sib_recv, own, part,
    x0_recv, s0, u0_recv, v0_recv, u1_recv, s1, x1_recv, v1_recv,
    wo_part, wo_send, wo_recv, wo_rs, wox_recv, wou_src, wou_recv, wov_recv,
    sm_c, sm_x, sm_u, sm_v,
    local_sems, send_sems, recv_sems,
):
    member, grid = lax.axis_index("member"), lax.axis_index("grid")
    c, zlo = member % 2, member // 2
    a, b = zlo // 2, zlo % 2
    zhi, y, x = grid % 2, (grid // 2) % 8, grid // 16
    z = zhi * 4 + zlo
    u = y * (1 - c) + z * c
    v = z * (1 - c) + y * c

    def device(x, y, z, c):
        return ((z % 4) * 2 + c, (x * 8 + y) * 2 + z // 4)

    def to_x(k):
        return device((x + k) % 4, y, z, c)

    def to_u(k):
        return device(x, (y + k * (1 - c)) % 8, (z + k * c) % 8, c)

    def to_v(k):
        return device(x, (y + k * c) % 8, (z + k * (1 - c)) % 8, c)

    sibling = (zlo * 2 + 1 - c, grid)

    def flip(bit, by):
        return 1 - bit if by else bit

    def member_of(rel):
        ra, rb, rc = rel
        return (2 * flip(a, ra) + flip(b, rb)) * 2 + flip(c, rc)

    rels = [(ra, rb, rc) for ra in (1, 0) for rb in (1, 0) for rc in (1, 0)][:-1]

    started = []

    def send(src, dst, to):
        i = len(started)
        copy = pltpu.make_async_remote_copy(
            src_ref=src, dst_ref=dst, send_sem=send_sems.at[i], recv_sem=recv_sems.at[i],
            device_id=to, device_id_type=MESH,
        )
        copy.start()
        started.append(copy)
        return copy

    def arrived(copies):
        for copy in copies:
            copy.wait_recv()

    barrier = pltpu.get_barrier_semaphore()
    partners = (
        [(member_of(rel), grid) for rel in rels]
        + [to_x(k) for k in FAR4] + [to_u(k) for k in FAR8] + [to_v(k) for k in FAR8]
    )
    for partner in partners:
        pl.semaphore_signal(barrier, inc=1, device_id=partner, device_id_type=MESH)

    halves = [1 - a, a]
    load_w = [
        pltpu.make_async_copy(
            win_hbm.at[pl.ds(512 * i, 512)], win.at[pl.ds(512 * i, 512)], local_sems.at[i])
        for i in range(2)
    ]
    load_l = [
        pltpu.make_async_copy(
            lat_hbm.at[0, :, pl.ds(pl.multiple_of(h * 256, 256), 256)],
            lat.at[:, pl.ds(pl.multiple_of(h * 256, 256), 256)], local_sems.at[2 + i])
        for i, h in enumerate(halves)
    ]
    for copy in load_w + load_l:
        copy.start()

    for i in range(4):
        bias[pl.ds(128 * i, 128), :] = jnp.transpose(
            jnp.broadcast_to(bin_ref[:, pl.ds(128 * i, 128)], (128, 128)))
    wop[...] = jnp.zeros_like(wop)
    wop[:, 0:VARS] = wo_ref[...]
    wop_t[...] = jnp.transpose(wop[...])
    row[...] = jnp.zeros_like(row)
    row[:, 0:VARS] = bo_ref[...]
    bias_out = jnp.transpose(jnp.broadcast_to(row[...], (128, 128)))[0:2 * FOLD]
    lane = lax.broadcasted_iota(jnp.int32, (FOLD, 128), 1)
    low_lane = lane < 64
    low_row = lax.broadcasted_iota(jnp.int32, (1, 128), 1) < 64

    def swap(value):
        return pltpu.roll(value, 64, 1)

    for i in range(2):
        load_w[i].wait()
        for r in range(2):
            at = 512 * i + 256 * r
            win_t[:, pl.ds(at, 256)] = jnp.transpose(win[pl.ds(at, 256), :])

    f_copies = []
    for i, h in enumerate(halves):
        cols = pl.ds(pl.multiple_of(h * 256, 256), 256)
        load_l[i].wait()
        pre[:, cols] = dot(win_t[...], lat[:, cols])

        def activate(r, _):
            rows = pl.ds(pl.multiple_of(r * 64, 64), 64)
            shift = bias[rows, :]
            value = pre[rows, cols] + jnp.concatenate([shift, shift], axis=1)
            pre[rows, cols] = value
            inner = GELU_A * (value + GELU_B * (value * value * value))
            hidden[rows, cols] = (0.5 * value * (1.0 + jnp.tanh(inner))).astype(BF16)
            return 0

        lax.fori_loop(0, HID // 64, activate, 0)
        field = dot(wop_t[0:2 * FOLD, :], hidden[:, cols])
        for t in range(2):
            chunk = (field[:, 128 * t:128 * t + 128] + bias_out).astype(BF16).astype(F32)
            lo, hi = chunk[0:FOLD], chunk[FOLD:2 * FOLD]
            f_send[i, t, 0] = jnp.where(low_lane, lo, swap(hi)).astype(BF16)
            f_send[i, t, 1] = jnp.where(low_lane, swap(lo), hi).astype(BF16)
        if i == 0:
            pl.semaphore_wait(barrier, len(partners))
        for rel in rels:
            if rel[0] == 1 - i:
                src = f_send.at[i, flip(b, rel[1]), flip(c, rel[2])]
                f_copies.append(send(src, f_recv.at[member], (member_of(rel), grid)))
    f_recv[pl.ds(member, 1)] = f_send[1, pl.ds(b, 1), pl.ds(c, 1)].reshape(1, FOLD, 128)

    def derive(r, _):
        rows = pl.ds(pl.multiple_of(r * 32, 32), 32)
        value = pre[rows, :]
        square = value * value
        t = jnp.tanh(GELU_A * (value + GELU_B * (value * square)))
        dgelu[rows, :] = 0.5 * (1.0 + t) + (0.5 * GELU_A) * value * (1.0 - t * t) * (
            1.0 + (3.0 * GELU_B) * square)
        return 0

    lax.fori_loop(0, HID // 32, derive, 0)
    obs_pad[...] = jnp.zeros_like(obs_pad)
    own_cols = pl.ds(pl.multiple_of(zlo * 128, 128), 128)
    obs_pad[0:VARS, :] = obs_ref[:, own_cols]
    lo, hi = obs_pad[0:FOLD], obs_pad[FOLD:2 * FOLD]
    first = c == 0
    observed = jnp.where(low_lane, jnp.where(first, lo, swap(lo)), jnp.where(first, swap(hi), hi))
    area = area_ref[:, own_cols]
    area = jnp.where(low_row, jnp.where(first, area, swap(area)), jnp.where(first, swap(area), area))
    factor = area * (VARS * math.sqrt(8 / total_columns))
    gl[2 * FOLD:128, :] = jnp.zeros((128 - 2 * FOLD, COLS), BF16)

    def norm(difference):
        total = jnp.sum(difference * difference, axis=0, keepdims=True)
        square = (total + swap(total)) / VARS + EPSILON
        inverse = lax.rsqrt(square)
        return square * inverse, inverse

    arrived(f_copies)
    fields = [f_recv[i].astype(F32) for i in range(8)]
    grads = []
    true_total = jnp.zeros((1, 128), F32)
    for m in range(8):
        difference = fields[m] - observed
        distance, inverse = norm(difference)
        true_total = true_total + distance
        grads.append(difference * (factor * inverse * (1.0 / (VARS * 8))))
    pair_total = jnp.full((1, 128), 8.0 * math.sqrt(EPSILON), F32)
    for m in range(8):
        for n in range(m + 1, 8):
            difference = fields[m] - fields[n]
            distance, inverse = norm(difference)
            pair_total = pair_total + 2.0 * distance
            pull = difference * (factor * inverse * (1.0 / (VARS * 64)))
            grads[m] = grads[m] - pull
            grads[n] = grads[n] + pull
    for m in range(8):
        g_send[m] = grads[m].astype(BF16)
    g_copies = []
    for rel in rels:
        there = member_of(rel)
        g_copies.append(send(g_send.at[there], g_recv.at[member], (there, grid)))
    g_recv[pl.ds(member, 1)] = g_send[pl.ds(member, 1)]
    loss = true_total * (1.0 / 8) - pair_total * (1.0 / 128)
    loss_recv[pl.ds(member, 1)] = jnp.broadcast_to(loss, (1, 8, 128))
    loss_copies = [
        send(loss_recv.at[member], loss_recv.at[member], (member_of(rel), grid)) for rel in rels]

    arrived(g_copies)
    for t in range(4):
        left, right = g_recv[2 * t].astype(F32), g_recv[2 * t + 1].astype(F32)
        cols = pl.ds(128 * t, 128)
        gl[0:FOLD, cols] = jnp.where(low_lane, left, swap(right)).astype(BF16)
        gl[FOLD:2 * FOLD, cols] = jnp.where(low_lane, swap(left), right).astype(BF16)

    def grad_hidden(r, _):
        rows = pl.ds(pl.multiple_of(r * 128, 128), 128)
        gp[rows, :] = (dot(wop[rows, :], gl[...]) * dgelu[rows, :]).astype(BF16)
        return 0

    lax.fori_loop(0, HID // 128, grad_hidden, 0)

    sib_copies = [None, None]
    for q in (1, 0):
        rows = pl.ds(pl.multiple_of((1 - c) * 512 + q * 256, 256), 256)
        sib_send[q] = dot_nt(lat[rows, :], gp[...]).astype(BF16)
        sib_copies[q] = send(sib_send.at[q], sib_recv.at[q], sibling)
    wo_part[...] = dot_nt(hidden[...], gl[...])
    wo_send[...] = wo_part[pl.ds(pl.multiple_of((1 - c) * 256, 256), 256), :].astype(BF16)
    wo_copy = send(wo_send, wo_recv, sibling)
    ones = jnp.ones((16, COLS), BF16)
    sum_in = dot_nt(ones, gp[...])[0:1]
    sum_out = dot_nt(ones, gl[...])[0:1]
    rows8 = lax.broadcasted_iota(jnp.int32, (8, 128), 0)
    tile = jnp.where(rows8 == 4, sum_out, 0.0)
    for i in range(4):
        tile = jnp.where(rows8 == i, sum_in[:, 128 * i:128 * i + 128], tile)
    sm_c[pl.ds(c, 1)] = tile.reshape(1, 8, 128)
    smc_copy = send(sm_c.at[c], sm_c.at[c], sibling)

    x_cols = pl.ds(pl.multiple_of(x * 128, 128), 128)
    u_rows = pl.ds(pl.multiple_of(u * 32, 32), 32)

    def own_half(q):
        rows = pl.ds(pl.multiple_of(c * 512 + q * 256, 256), 256)
        own[q] = dot_nt(lat[rows, :], gp[...])

    def merge(q):
        sib_copies[q].wait_recv()
        part[q] = (own[q] + sib_recv[q].astype(F32)).astype(BF16)

    own_half(1)
    merge(1)
    u1_copies = []
    for k in FAR8:
        rows = pl.ds(pl.multiple_of((u + k) % 8 * 32, 32), 32)
        u1_copies.append(send(part.at[1, rows], u1_recv.at[k - 1], to_u(k)))
    own_half(0)
    merge(0)
    x0_copies = []
    for k in FAR4:
        cols = pl.ds(pl.multiple_of((x + k) % 4 * 128, 128), 128)
        x0_copies.append(send(part.at[0, :, cols], x0_recv.at[k - 1], to_x(k)))
    wo_copy.wait_recv()
    wo_rs[...] = (
        wo_part[pl.ds(pl.multiple_of(c * 256, 256), 256), :] + wo_recv[...].astype(F32)).astype(BF16)
    wox_copies = []
    for k in FAR4:
        rows = pl.ds(pl.multiple_of((x + k) % 4 * 64, 64), 64)
        wox_copies.append(send(wo_rs.at[rows], wox_recv.at[k - 1], to_x(k)))
    smc_copy.wait_recv()
    sm_x[pl.ds(x, 1)] = (sm_c[0] + sm_c[1]).reshape(1, 8, 128)
    smx_copies = [send(sm_x.at[x], sm_x.at[x], to_x(k)) for k in FAR4]

    arrived(x0_copies)
    total = part[0, :, x_cols].astype(F32)
    for k in range(3):
        total = total + x0_recv[k].astype(F32)
    s0[...] = total.astype(BF16)
    u0_copies = []
    for k in FAR8:
        rows = pl.ds(pl.multiple_of((u + k) % 8 * 32, 32), 32)
        u0_copies.append(send(s0.at[rows], u0_recv.at[k - 1], to_u(k)))
    arrived(wox_copies)
    total = wo_rs[pl.ds(pl.multiple_of(x * 64, 64), 64), :].astype(F32)
    for k in range(3):
        total = total + wox_recv[k].astype(F32)
    wou_src[...] = total
    wou_copies = []
    for k in FAR8:
        rows = pl.ds(pl.multiple_of((u + k) % 8 * 8, 8), 8)
        wou_copies.append(send(wou_src.at[rows], wou_recv.at[k - 1], to_u(k)))
    arrived(smx_copies)
    sm_u[pl.ds(u, 1)] = (sm_x[0] + sm_x[1] + sm_x[2] + sm_x[3]).reshape(1, 8, 128)
    smu_copies = [send(sm_u.at[u], sm_u.at[u], to_u(k)) for k in FAR8]
    arrived(u1_copies)
    total = part[1, u_rows, :].astype(F32)
    for k in range(7):
        total = total + u1_recv[k].astype(F32)
    s1[...] = total.astype(BF16)
    x1_copies = []
    for k in FAR4:
        cols = pl.ds(pl.multiple_of((x + k) % 4 * 128, 128), 128)
        x1_copies.append(send(s1.at[:, cols], x1_recv.at[k - 1], to_x(k)))

    arrived(x1_copies)
    total = s1[:, x_cols].astype(F32)
    for k in range(3):
        total = total + x1_recv[k].astype(F32)
    v1_recv[pl.ds(v, 1)] = total.astype(BF16).reshape(1, 32, 128)
    v1_copies = [send(v1_recv.at[v], v1_recv.at[v], to_v(k)) for k in FAR8]
    arrived(u0_copies)
    total = s0[u_rows, :].astype(F32)
    for k in range(7):
        total = total + u0_recv[k].astype(F32)
    v0_recv[pl.ds(v, 1)] = total.astype(BF16).reshape(1, 32, 128)
    v0_copies = [send(v0_recv.at[v], v0_recv.at[v], to_v(k)) for k in FAR8]
    arrived(wou_copies)
    total = wou_src[pl.ds(pl.multiple_of(u * 8, 8), 8), :]
    for k in range(7):
        total = total + wou_recv[k]
    wov_recv[pl.ds(v, 1)] = total.reshape(1, 8, 128)
    wov_copies = [send(wov_recv.at[v], wov_recv.at[v], to_v(k)) for k in FAR8]
    arrived(smu_copies)
    total = sm_u[0]
    for k in range(1, 8):
        total = total + sm_u[k]
    sm_v[pl.ds(v, 1)] = total.reshape(1, 8, 128)
    smv_copies = [send(sm_v.at[v], sm_v.at[v], to_v(k)) for k in FAR8]

    base = c * 512

    def block(q, rows_at, rows, cols):
        return gw_ref.at[pl.ds(pl.multiple_of(base + q * 256 + rows_at, 32), rows), cols]

    arrived(v1_copies)
    total = v1_recv[0].astype(F32)
    for k in range(1, 8):
        total = total + v1_recv[k].astype(F32)
    spot = block(1, u * 32, 32, x_cols)
    spot[...] = total.astype(BF16)
    x1_copies = [send(spot, spot, to_x(k)) for k in FAR4]
    arrived(v0_copies)
    total = v0_recv[0].astype(F32)
    for k in range(1, 8):
        total = total + v0_recv[k].astype(F32)
    spot = block(0, u * 32, 32, x_cols)
    spot[...] = total.astype(BF16)
    u0_copies = [send(spot, spot, to_u(k)) for k in FAR8]
    arrived(wov_copies)
    total = wov_recv[0]
    for k in range(1, 8):
        total = total + wov_recv[k]
    spot = gwo_ref.at[pl.ds(pl.multiple_of(c * 256 + x * 64 + u * 8, 8), 8)]
    spot[...] = total
    wou_copies = [send(spot, spot, to_u(k)) for k in FAR8]
    arrived(smv_copies)
    total = sm_v[0]
    for k in range(1, 8):
        total = total + sm_v[k]
    small_ref[...] = total

    arrived(x1_copies)
    spot = block(1, u * 32, 32, pl.ds(0, 512))
    u1_copies = [send(spot, spot, to_u(k)) for k in FAR8]
    last = [send(spot, spot, sibling)]
    arrived(u0_copies)
    spot = block(0, 0, 256, x_cols)
    x0_copies = [send(spot, spot, to_x(k)) for k in FAR4]
    last.append(send(spot, spot, sibling))
    arrived(wou_copies)
    spot = gwo_ref.at[pl.ds(pl.multiple_of(c * 256 + x * 64, 64), 64)]
    wox_copies = [send(spot, spot, to_x(k)) for k in FAR4]
    last.append(send(spot, spot, sibling))

    for k, copy in zip(FAR4, x0_copies):
        copy.wait_recv()
        cols = pl.ds(pl.multiple_of((x + 4 - k) % 4 * 128, 128), 128)
        spot = block(0, 0, 256, cols)
        last.append(send(spot, spot, sibling))
    for k, copy in zip(FAR4, wox_copies):
        copy.wait_recv()
        spot = gwo_ref.at[pl.ds(pl.multiple_of(c * 256 + (x + 4 - k) % 4 * 64, 64), 64)]
        last.append(send(spot, spot, sibling))
    for k, copy in zip(FAR8, u1_copies):
        copy.wait_recv()
        spot = block(1, (u + 8 - k) % 8 * 32, 32, pl.ds(0, 512))
        last.append(send(spot, spot, sibling))

    arrived(loss_copies)
    for t in range(4):
        loss_ref[t:t + 1, :] = jnp.where(
            low_row, loss_recv[2 * t, 0:1, :], loss_recv[2 * t + 1, 0:1, :])
    arrived(last)
    for copy in started:
        copy.wait_send()


def per_device(latent, w_in, b_in, output_weight, output_bias, observed_field, area):
    total_columns = latent.shape[2] * lax.axis_size("grid")
    vmem = pl.BlockSpec(memory_space=pltpu.VMEM)
    hbm = pl.BlockSpec(memory_space=pl.ANY)

    def scratch(dtype, *shape):
        return pltpu.VMEM(shape, dtype)

    loss, grad_w_in, small, grad_w_out = pl.pallas_call(
        lambda *refs: kernel(total_columns, *refs),
        out_shape=(
            jax.ShapeDtypeStruct((4, 128), F32),
            jax.ShapeDtypeStruct((DIN, HID), BF16),
            jax.ShapeDtypeStruct((8, 128), F32),
            jax.ShapeDtypeStruct((HID, 128), F32),
        ),
        in_specs=[hbm, hbm, vmem, vmem, vmem, vmem, vmem],
        out_specs=(vmem, vmem, vmem, vmem),
        scratch_shapes=[
            scratch(BF16, DIN, COLS), scratch(BF16, DIN, HID), scratch(BF16, HID, DIN),
            scratch(F32, HID, 128), scratch(F32, HID, COLS), scratch(F32, HID, COLS),
            scratch(BF16, HID, COLS), scratch(BF16, HID, 128), scratch(BF16, 128, HID),
            scratch(F32, 1, 128), scratch(F32, 2 * FOLD, 128),
            scratch(BF16, 2, 2, 2, FOLD, 128), scratch(BF16, 8, FOLD, 128),
            scratch(BF16, 8, FOLD, 128), scratch(BF16, 8, FOLD, 128),
            scratch(F32, 8, 8, 128), scratch(BF16, 128, COLS), scratch(BF16, HID, COLS),
            scratch(BF16, 2, 256, HID), scratch(BF16, 2, 256, HID),
            scratch(F32, 2, 256, HID), scratch(BF16, 2, 256, HID),
            scratch(BF16, 3, 256, 128), scratch(BF16, 256, 128),
            scratch(BF16, 7, 32, 128), scratch(BF16, 8, 32, 128),
            scratch(BF16, 7, 32, HID), scratch(BF16, 32, HID),
            scratch(BF16, 3, 32, 128), scratch(BF16, 8, 32, 128),
            scratch(F32, HID, 128), scratch(BF16, 256, 128), scratch(BF16, 256, 128),
            scratch(BF16, 256, 128), scratch(BF16, 3, 64, 128),
            scratch(F32, 64, 128), scratch(F32, 7, 8, 128), scratch(F32, 8, 8, 128),
            scratch(F32, 2, 8, 128), scratch(F32, 4, 8, 128),
            scratch(F32, 8, 8, 128), scratch(F32, 8, 8, 128),
            pltpu.SemaphoreType.DMA((4,)),
            pltpu.SemaphoreType.DMA((N_SEMS,)), pltpu.SemaphoreType.DMA((N_SEMS,)),
        ],
        compiler_params=pltpu.CompilerParams(
            collective_id=0, has_side_effects=True, vmem_limit_bytes=40 * 2**20),
        cost_estimate=pl.CostEstimate(
            flops=4 * DIN * HID * COLS, bytes_accessed=4 * 2**20, transcendentals=2 * HID * COLS),
        name="energy_score_step",
    )(
        latent, w_in, b_in.reshape(1, HID), output_weight, output_bias.reshape(1, VARS),
        observed_field, area.reshape(1, COLS),
    )
    return (
        loss.reshape(COLS), grad_w_in, small[0:4].reshape(HID), grad_w_out[:, 0:VARS],
        small[4, 0:VARS],
    )


def solution(mesh):
    placed = (P("member", None, "grid"), P(), P(), P(), P(), P(None, "grid"), P("grid"))
    return jax.shard_map(
        per_device,
        mesh=mesh,
        in_specs=placed,
        out_specs=(P("grid"), P(), P(), P(), P()),
        check_vma=False,
    )
```

time: 306 us -> 65.6 us (0.21)
  blocking collectives: 147 us -> 0 us
  waiting for transfers between devices: 134 us -> 0 us
  Pallas kernels: 0 us -> 57.6 us
  between operations: 14.1 us -> 0.71 us
  matrix products: 5.11 us -> 0 us
    psum x1 -> x0, waiting for transfers between devices: 134 us -> none  [per_device(): lax.psum((part_w_in, part_b_in, part_w_out, part_b_out), ('member', 'grid'))]
    psum x2 -> x0, blocking collectives: 125 us -> none  [the longest x1 111 us: per_device(): lax.psum((part_w_in, part_b_in, part_w_out, part_b_out), ('member', 'grid'))]
    pallas_call x0 -> x1, Pallas kernels: none -> 57.6 us  [per_device(): pl.pallas_call(lambda *refs: kernel(total_columns, *refs), out_shape=(jax...]
    all_gather x1 -> x0, blocking collectives: 22.3 us -> none  [per_device(): lax.all_gather(lone_run_field[None], 'member', axis=0, tiled=True)]
    dot_general x5 -> x0, matrix products: 5.11 us -> none  [the longest x1 2.26 us: per_device(): jnp.dot(w_in.T, latent_cols, preferred_element_type=jnp.float32)]
  transfers between devices with their start and end apart: 1 -> 0, of which waited for: 1 -> 0; matrix products, arithmetic and copies ran while one was open for 1% -> 0% of each run, Pallas kernels for 0% -> 0%
where the time goes in v1:
time: 65.6 us; the launch traced here: 65.4 us
  Pallas kernels  57.6 us (88%)
  local copies, waits for them, and re-layouts  7.03 us (11%)
  between operations  0.71 us (1%)
    pallas_call x1, Pallas kernels, per_device(): pl.pallas_call(lambda *refs: kernel(total_columns, *refs), out_shape=(jax...  57.6 us
    unnamed x16, local copies, waits for them, and re-layouts  5.93 us

profile of v1, /device:TPU:1, one launch (start us, length us, event | category | flops | bytes accessed | tf_op | source)
XLA Modules:
  0.0 65.4 jit_solution(12732864051447132375)
XLA Ops:
  0.6 0.0 copy-start.2
  0.6 0.0 copy-start.3
  0.7 0.0 copy-start.4
  0.7 0.0 copy-start.5
  0.7 1.1 %copy.12.refs_3_ = bf16[512,83]{1,0:T(8,128)(2,1)S(1)} copy(bf16[512,83]{0,1:T(8,128)(2,1)} %param.10) | data formatting | bytes 169984 | tf_op args[3]
  1.8 0.0 copy-done.2
  1.8 0.0 copy-done.3
  1.8 0.0 copy-done.4
  1.8 0.0 copy-done.5
  1.8 0.0 copy-start
  1.8 1.2 %copy-done = bf16[1,1024,512]{2,1,0:T(8,128)(2,1)S(1)} copy-done((bf16[1,1024,512]{2,1,0:T(8,128)(2,1)S(1)}, bf16[1,1024,512]{2,1,0:T(8,128)(2,1)}, u32[]{:S(2)}) %copy-start) | copy-done | bytes 1048600
  3.1 0.0 copy-start.1
  3.1 1.2 %copy-done.1 = bf16[1024,512]{1,0:T(8,128)(2,1)S(1)} copy-done((bf16[1024,512]{1,0:T(8,128)(2,1)S(1)}, bf16[1024,512]{1,0:T(8,128)(2,1)}, u32[]{:S(2)}) %copy-start.1) | copy-done | bytes 1048600
  4.3 57.6 %energy_score_step.1 = (f32[4,128]{1,0:T(4,128)S(1)}, bf16[1024,512]{1,0:T(8,128)(2,1)S(1)}, f32[8,128]{1,0:T(8,128)S(1)}, f32[512,128]{1,0:T(8,128)S(1)}) custom-call(bf16[1,1024,512]{2,1,0:T(8,128)(2,1)S(1)} %copy-done, bf16[1024,512]{1,0:T(8,128)(2,1)S(1)} %copy-done.1, f32[1,512]{1,0:T(1,128)S(1)} %bitcast.11, bf16[512,83]{1,0:T(8,128)(2,1)S(1)} %copy.12.refs_3_, ...), custom_call_target="tpu_custom_call" | custom-call | flops 1073741824 | bytes 4194304 | tf_op jit(solution)/shard_map/energy_score_step/pallas_call | solution.py:423
  61.9 0.5 slice_bitcast_fusion.1
  62.4 0.6 slice_bitcast_fusion
  63.0 0.8 %copy.13 = f32[512,83]{0,1:T(8,128)} copy(f32[512,83]{1,0:T(8,128)S(1)} %bitcast.9) | data formatting | bytes 339968
  63.8 0.6 copy.16
  64.4 1.0 %copy.17 = bf16[1024,512]{1,0:T(8,128)(2,1)} copy(bf16[1024,512]{1,0:T(8,128)(2,1)S(1)} %get-tuple-element.24) | data formatting | bytes 2097152
Async XLA Ops:
  0.6 1.2 %copy-start.2 = (f32[83,512]{1,0:T(8,128)S(1)}, f32[83,512]{1,0:T(8,128)}, u32[]{:S(2)}) copy-start(f32[83,512]{1,0:T(8,128)} %refs_5_.1) | copy-start | bytes 509956
  0.6 1.2 %copy-start.3 = (f32[512]{0:T(512)S(1)}, f32[512]{0:T(512)}, u32[]{:S(2)}) copy-start(f32[512]{0:T(512)} %param.9) | copy-start | bytes 6148
  0.7 1.2 %copy-start.4 = (f32[512]{0:T(512)S(1)}, f32[512]{0:T(512)}, u32[]{:S(2)}) copy-start(f32[512]{0:T(512)} %param.13) | copy-start | bytes 6148
  0.7 1.2 %copy-start.5 = (f32[83]{0:T(128)S(1)}, f32[83]{0:T(128)}, u32[]{:S(2)}) copy-start(f32[83]{0:T(128)} %param.11) | copy-start | bytes 1000
  1.8 1.2 %copy-start = (bf16[1,1024,512]{2,1,0:T(8,128)(2,1)S(1)}, bf16[1,1024,512]{2,1,0:T(8,128)(2,1)}, u32[]{:S(2)}) copy-start(bf16[1,1024,512]{2,1,0:T(8,128)(2,1)} %refs_0_.1) | copy-start | bytes 3145732
  3.1 1.2 %copy-start.1 = (bf16[1024,512]{1,0:T(8,128)(2,1)S(1)}, bf16[1024,512]{1,0:T(8,128)(2,1)}, u32[]{:S(2)}) copy-start(bf16[1024,512]{1,0:T(8,128)(2,1)} %refs_1_.1) | copy-start | bytes 3145732

commit v2 on v1

--- a/solution.py
+++ b/solution.py
@@ -31,16 +31,21 @@
     return lax.dot_general(a, b, (((1,), (1,)), ((), ())), preferred_element_type=F32)
 
 
+def dot_tn(a, b):
+    return lax.dot_general(a, b, (((0,), (0,)), ((), ())), preferred_element_type=F32)
+
+
 def kernel(
     total_columns,
-    lat_hbm, win_hbm, bin_ref, wo_ref, bo_ref, obs_ref, area_ref,
-    loss_ref, gw_ref, small_ref, gwo_ref,
-    lat, win, win_t, bias, pre, dgelu, hidden, wop, wop_t, row, obs_pad,
+    lat_hbm, win_hbm, bin_hbm, wo_hbm, bo_hbm, obs_hbm, area_hbm,
+    loss_ref, gw_ref, gbin_ref, gwo_ref, gbo_ref,
+    bin_ref, wo_ref, bo_ref, obs_ref, area_ref, gwo,
+    lat, win, bias, pre, dgelu, hidden, wop, wop_t, row, obs_pad,
     f_send, f_recv, g_send, g_recv, loss_recv, gl, gp,
     sib_send, sib_recv, own, part,
-    x0_recv, s0, u0_recv, v0_recv, u1_recv, s1, x1_recv, v1_recv,
+    x0_recv, s0, u0_recv, u1_recv, s1, x1_recv, v_recv,
     wo_part, wo_send, wo_recv, wo_rs, wox_recv, wou_src, wou_recv, wov_recv,
-    sm_c, sm_x, sm_u, sm_v,
+    sm_c, sm_x,
     local_sems, send_sems, recv_sems,
 ):
     member, grid = lax.axis_index("member"), lax.axis_index("grid")
@@ -74,7 +79,12 @@
 
     rels = [(ra, rb, rc) for ra in (1, 0) for rb in (1, 0) for rc in (1, 0)][:-1]
 
-    started = []
+    started, fences = [], [0, 0]
+
+    def drain():
+        for copy in started[fences[-2]:fences[-1]]:
+            copy.wait_send()
+        fences.append(len(started))
 
     def send(src, dst, to):
         i = len(started)
@@ -110,16 +120,23 @@
             lat.at[:, pl.ds(pl.multiple_of(h * 256, 256), 256)], local_sems.at[2 + i])
         for i, h in enumerate(halves)
     ]
-    for copy in load_w + load_l:
+    load_small = [
+        pltpu.make_async_copy(src, dst, local_sems.at[4 + i])
+        for i, (src, dst) in enumerate((
+            (bin_hbm, bin_ref), (wo_hbm, wo_ref), (bo_hbm, bo_ref),
+            (obs_hbm, obs_ref), (area_hbm, area_ref)))
+    ]
+    for copy in load_w + load_small[:3] + load_l + load_small[3:]:
         copy.start()
 
+    wop_t[...] = jnp.zeros_like(wop_t)
+    row[...] = jnp.zeros_like(row)
+    for copy in load_small[:3]:
+        copy.wait()
     for i in range(4):
         bias[pl.ds(128 * i, 128), :] = jnp.transpose(
             jnp.broadcast_to(bin_ref[:, pl.ds(128 * i, 128)], (128, 128)))
-    wop[...] = jnp.zeros_like(wop)
-    wop[:, 0:VARS] = wo_ref[...]
-    wop_t[...] = jnp.transpose(wop[...])
-    row[...] = jnp.zeros_like(row)
+    wop_t[0:VARS, :] = wo_ref[...]
     row[:, 0:VARS] = bo_ref[...]
     bias_out = jnp.transpose(jnp.broadcast_to(row[...], (128, 128)))[0:2 * FOLD]
     lane = lax.broadcasted_iota(jnp.int32, (FOLD, 128), 1)
@@ -129,20 +146,17 @@
     def swap(value):
         return pltpu.roll(value, 64, 1)
 
-    for i in range(2):
-        load_w[i].wait()
-        for r in range(2):
-            at = 512 * i + 256 * r
-            win_t[:, pl.ds(at, 256)] = jnp.transpose(win[pl.ds(at, 256), :])
+    for copy in load_w:
+        copy.wait()
 
     f_copies = []
     for i, h in enumerate(halves):
         cols = pl.ds(pl.multiple_of(h * 256, 256), 256)
         load_l[i].wait()
-        pre[:, cols] = dot(win_t[...], lat[:, cols])
+        pre[:, cols] = dot_tn(win[...], lat[:, cols])
 
         def activate(r, _):
-            rows = pl.ds(pl.multiple_of(r * 64, 64), 64)
+            rows = pl.ds(pl.multiple_of(r * 128, 128), 128)
             shift = bias[rows, :]
             value = pre[rows, cols] + jnp.concatenate([shift, shift], axis=1)
             pre[rows, cols] = value
@@ -150,7 +164,7 @@
             hidden[rows, cols] = (0.5 * value * (1.0 + jnp.tanh(inner))).astype(BF16)
             return 0
 
-        lax.fori_loop(0, HID // 64, activate, 0)
+        lax.fori_loop(0, HID // 128, activate, 0)
         field = dot(wop_t[0:2 * FOLD, :], hidden[:, cols])
         for t in range(2):
             chunk = (field[:, 128 * t:128 * t + 128] + bias_out).astype(BF16).astype(F32)
@@ -166,7 +180,7 @@
     f_recv[pl.ds(member, 1)] = f_send[1, pl.ds(b, 1), pl.ds(c, 1)].reshape(1, FOLD, 128)
 
     def derive(r, _):
-        rows = pl.ds(pl.multiple_of(r * 32, 32), 32)
+        rows = pl.ds(pl.multiple_of(r * 128, 128), 128)
         value = pre[rows, :]
         square = value * value
         t = jnp.tanh(GELU_A * (value + GELU_B * (value * square)))
@@ -174,7 +188,10 @@
             1.0 + (3.0 * GELU_B) * square)
         return 0
 
-    lax.fori_loop(0, HID // 32, derive, 0)
+    lax.fori_loop(0, HID // 128, derive, 0)
+    wop[...] = jnp.transpose(wop_t[...])
+    for copy in load_small[3:]:
+        copy.wait()
     obs_pad[...] = jnp.zeros_like(obs_pad)
     own_cols = pl.ds(pl.multiple_of(zlo * 128, 128), 128)
     obs_pad[0:VARS, :] = obs_ref[:, own_cols]
@@ -222,6 +239,7 @@
     loss_copies = [
         send(loss_recv.at[member], loss_recv.at[member], (member_of(rel), grid)) for rel in rels]
 
+    drain()
     arrived(g_copies)
     for t in range(4):
         left, right = g_recv[2 * t].astype(F32), g_recv[2 * t + 1].astype(F32)
@@ -288,6 +306,7 @@
     sm_x[pl.ds(x, 1)] = (sm_c[0] + sm_c[1]).reshape(1, 8, 128)
     smx_copies = [send(sm_x.at[x], sm_x.at[x], to_x(k)) for k in FAR4]
 
+    drain()
     arrived(x0_copies)
     total = part[0, :, x_cols].astype(F32)
     for k in range(3):
@@ -301,14 +320,13 @@
     total = wo_rs[pl.ds(pl.multiple_of(x * 64, 64), 64), :].astype(F32)
     for k in range(3):
         total = total + wox_recv[k].astype(F32)
-    wou_src[...] = total
-    wou_copies = []
-    for k in FAR8:
-        rows = pl.ds(pl.multiple_of((u + k) % 8 * 8, 8), 8)
-        wou_copies.append(send(wou_src.at[rows], wou_recv.at[k - 1], to_u(k)))
     arrived(smx_copies)
-    sm_u[pl.ds(u, 1)] = (sm_x[0] + sm_x[1] + sm_x[2] + sm_x[3]).reshape(1, 8, 128)
-    smu_copies = [send(sm_u.at[u], sm_u.at[u], to_u(k)) for k in FAR8]
+    small = sm_x[0] + sm_x[1] + sm_x[2] + sm_x[3]
+    for j in range(8):
+        wou_src[j, 0:8] = total[8 * j:8 * j + 8]
+        wou_src[j, 8:16] = small
+    wou_recv[pl.ds(u, 1)] = wou_src[pl.ds(u, 1)]
+    wou_copies = [send(wou_src.at[(u + k) % 8], wou_recv.at[u], to_u(k)) for k in FAR8]
     arrived(u1_copies)
     total = part[1, u_rows, :].astype(F32)
     for k in range(7):
@@ -323,58 +341,48 @@
     total = s1[:, x_cols].astype(F32)
     for k in range(3):
         total = total + x1_recv[k].astype(F32)
-    v1_recv[pl.ds(v, 1)] = total.astype(BF16).reshape(1, 32, 128)
-    v1_copies = [send(v1_recv.at[v], v1_recv.at[v], to_v(k)) for k in FAR8]
+    v_recv[v, 1] = total.astype(BF16)
     arrived(u0_copies)
     total = s0[u_rows, :].astype(F32)
     for k in range(7):
         total = total + u0_recv[k].astype(F32)
-    v0_recv[pl.ds(v, 1)] = total.astype(BF16).reshape(1, 32, 128)
-    v0_copies = [send(v0_recv.at[v], v0_recv.at[v], to_v(k)) for k in FAR8]
+    v_recv[v, 0] = total.astype(BF16)
+    v_copies = [send(v_recv.at[v], v_recv.at[v], to_v(k)) for k in FAR8]
     arrived(wou_copies)
-    total = wou_src[pl.ds(pl.multiple_of(u * 8, 8), 8), :]
-    for k in range(7):
+    total = wou_recv[0]
+    for k in range(1, 8):
         total = total + wou_recv[k]
-    wov_recv[pl.ds(v, 1)] = total.reshape(1, 8, 128)
+    wov_recv[pl.ds(v, 1)] = total.reshape(1, 16, 128)
     wov_copies = [send(wov_recv.at[v], wov_recv.at[v], to_v(k)) for k in FAR8]
-    arrived(smu_copies)
-    total = sm_u[0]
-    for k in range(1, 8):
-        total = total + sm_u[k]
-    sm_v[pl.ds(v, 1)] = total.reshape(1, 8, 128)
-    smv_copies = [send(sm_v.at[v], sm_v.at[v], to_v(k)) for k in FAR8]
+    drain()
 
     base = c * 512
 
     def block(q, rows_at, rows, cols):
         return gw_ref.at[pl.ds(pl.multiple_of(base + q * 256 + rows_at, 32), rows), cols]
 
-    arrived(v1_copies)
-    total = v1_recv[0].astype(F32)
+    arrived(v_copies)
+    total = v_recv[0].astype(F32)
     for k in range(1, 8):
-        total = total + v1_recv[k].astype(F32)
-    spot = block(1, u * 32, 32, x_cols)
-    spot[...] = total.astype(BF16)
-    x1_copies = [send(spot, spot, to_x(k)) for k in FAR4]
-    arrived(v0_copies)
-    total = v0_recv[0].astype(F32)
-    for k in range(1, 8):
-        total = total + v0_recv[k].astype(F32)
-    spot = block(0, u * 32, 32, x_cols)
-    spot[...] = total.astype(BF16)
-    u0_copies = [send(spot, spot, to_u(k)) for k in FAR8]
+        total = total + v_recv[k].astype(F32)
+    total = total.astype(BF16)
+    spot1 = block(1, u * 32, 32, x_cols)
+    spot1[...] = total[1]
+    spot0 = block(0, u * 32, 32, x_cols)
+    spot0[...] = total[0]
+    u0_copies = [send(spot0, spot0, to_u(k)) for k in FAR8]
+    x1_copies = [send(spot1, spot1, to_x(k)) for k in FAR4]
     arrived(wov_copies)
     total = wov_recv[0]
     for k in range(1, 8):
         total = total + wov_recv[k]
-    spot = gwo_ref.at[pl.ds(pl.multiple_of(c * 256 + x * 64 + u * 8, 8), 8)]
-    spot[...] = total
+    spot = gwo.at[pl.ds(pl.multiple_of(c * 256 + x * 64 + u * 8, 8), 8)]
+    spot[...] = total[0:8]
     wou_copies = [send(spot, spot, to_u(k)) for k in FAR8]
-    arrived(smv_copies)
-    total = sm_v[0]
-    for k in range(1, 8):
-        total = total + sm_v[k]
-    small_ref[...] = total
+    for i in range(4):
+        gbin_ref[:, 128 * i:128 * i + 128] = total[8 + i:9 + i]
+    gbo_ref[...] = total[12:13, 0:VARS]
+    drain()
 
     arrived(x1_copies)
     spot = block(1, u * 32, 32, pl.ds(0, 512))
@@ -385,53 +393,77 @@
     x0_copies = [send(spot, spot, to_x(k)) for k in FAR4]
     last.append(send(spot, spot, sibling))
     arrived(wou_copies)
-    spot = gwo_ref.at[pl.ds(pl.multiple_of(c * 256 + x * 64, 64), 64)]
+    spot = gwo.at[pl.ds(pl.multiple_of(c * 256 + x * 64, 64), 64)]
     wox_copies = [send(spot, spot, to_x(k)) for k in FAR4]
-    last.append(send(spot, spot, sibling))
-
-    for k, copy in zip(FAR4, x0_copies):
-        copy.wait_recv()
-        cols = pl.ds(pl.multiple_of((x + 4 - k) % 4 * 128, 128), 128)
-        spot = block(0, 0, 256, cols)
-        last.append(send(spot, spot, sibling))
-    for k, copy in zip(FAR4, wox_copies):
-        copy.wait_recv()
-        spot = gwo_ref.at[pl.ds(pl.multiple_of(c * 256 + (x + 4 - k) % 4 * 64, 64), 64)]
-        last.append(send(spot, spot, sibling))
-    for k, copy in zip(FAR8, u1_copies):
-        copy.wait_recv()
-        spot = block(1, (u + 8 - k) % 8 * 32, 32, pl.ds(0, 512))
-        last.append(send(spot, spot, sibling))
-
+    last_wo = [send(spot, spot, sibling)]
+
+    drain()
     arrived(loss_copies)
     for t in range(4):
-        loss_ref[t:t + 1, :] = jnp.where(
+        loss_ref[:, 128 * t:128 * t + 128] = jnp.where(
             low_row, loss_recv[2 * t, 0:1, :], loss_recv[2 * t + 1, 0:1, :])
+
+    for k, copy in reversed(list(zip(FAR4, wox_copies))):
+        copy.wait_recv()
+        spot = gwo.at[pl.ds(pl.multiple_of(c * 256 + (x + 4 - k) % 4 * 64, 64), 64)]
+        last_wo.append(send(spot, spot, sibling))
+    near_u = [(k, copy, u1_copies) for k, copy in zip(FAR8, u1_copies)][::-1]
+    near_x = [(k, copy, x0_copies) for k, copy in zip(FAR4, x0_copies)][::-1]
+    for k, copy, group in near_u[:4] + near_x[:2] + near_u[4:] + near_x[2:]:
+        copy.wait_recv()
+        if group is x0_copies:
+            cols = pl.ds(pl.multiple_of((x + 4 - k) % 4 * 128, 128), 128)
+            spot = block(0, 0, 256, cols)
+        else:
+            spot = block(1, (u + 8 - k) % 8 * 32, 32, pl.ds(0, 512))
+        last.append(send(spot, spot, sibling))
+    arrived(last_wo)
+    gwo_ref[...] = jnp.transpose(gwo[...])[0:VARS]
     arrived(last)
-    for copy in started:
-        copy.wait_send()
+    drain()
+    drain()
+
+
+def deliver(*refs):
+    results, places, sems = refs[0:5], refs[5:10], refs[10]
+    copies = [
+        pltpu.make_async_copy(src, dst, sems.at[i])
+        for i, (src, dst) in enumerate(zip(results, places))
+    ]
+    for copy in copies:
+        copy.start()
+    for copy in copies:
+        copy.wait()
 
 
 def per_device(latent, w_in, b_in, output_weight, output_bias, observed_field, area):
     total_columns = latent.shape[2] * lax.axis_size("grid")
     vmem = pl.BlockSpec(memory_space=pltpu.VMEM)
-    hbm = pl.BlockSpec(memory_space=pl.ANY)
+    hbm = pl.BlockSpec(memory_space=pltpu.HBM)
 
     def scratch(dtype, *shape):
         return pltpu.VMEM(shape, dtype)
 
-    loss, grad_w_in, small, grad_w_out = pl.pallas_call(
+    results = (
+        jax.ShapeDtypeStruct((1, COLS), F32),
+        jax.ShapeDtypeStruct((DIN, HID), BF16),
+        jax.ShapeDtypeStruct((1, HID), F32),
+        jax.ShapeDtypeStruct((VARS, HID), F32),
+        jax.ShapeDtypeStruct((1, VARS), F32),
+    )
+    operands = (
+        latent, w_in, b_in.reshape(1, HID), output_weight.T, output_bias.reshape(1, VARS),
+        observed_field, area.reshape(1, COLS),
+    )
+    made = pl.pallas_call(
         lambda *refs: kernel(total_columns, *refs),
-        out_shape=(
-            jax.ShapeDtypeStruct((4, 128), F32),
-            jax.ShapeDtypeStruct((DIN, HID), BF16),
-            jax.ShapeDtypeStruct((8, 128), F32),
-            jax.ShapeDtypeStruct((HID, 128), F32),
-        ),
-        in_specs=[hbm, hbm, vmem, vmem, vmem, vmem, vmem],
-        out_specs=(vmem, vmem, vmem, vmem),
+        out_shape=results,
+        in_specs=[hbm] * 7,
+        out_specs=(vmem,) * 5,
         scratch_shapes=[
-            scratch(BF16, DIN, COLS), scratch(BF16, DIN, HID), scratch(BF16, HID, DIN),
+            scratch(F32, 1, HID), scratch(BF16, VARS, HID), scratch(F32, 1, VARS),
+            scratch(F32, VARS, COLS), scratch(F32, 1, COLS), scratch(F32, HID, 128),
+            scratch(BF16, DIN, COLS), scratch(BF16, DIN, HID),
             scratch(F32, HID, 128), scratch(F32, HID, COLS), scratch(F32, HID, COLS),
             scratch(BF16, HID, COLS), scratch(BF16, HID, 128), scratch(BF16, 128, HID),
             scratch(F32, 1, 128), scratch(F32, 2 * FOLD, 128),
@@ -441,15 +473,14 @@
             scratch(BF16, 2, 256, HID), scratch(BF16, 2, 256, HID),
             scratch(F32, 2, 256, HID), scratch(BF16, 2, 256, HID),
             scratch(BF16, 3, 256, 128), scratch(BF16, 256, 128),
-            scratch(BF16, 7, 32, 128), scratch(BF16, 8, 32, 128),
+            scratch(BF16, 7, 32, 128),
             scratch(BF16, 7, 32, HID), scratch(BF16, 32, HID),
-            scratch(BF16, 3, 32, 128), scratch(BF16, 8, 32, 128),
+            scratch(BF16, 3, 32, 128), scratch(BF16, 8, 2, 32, 128),
             scratch(F32, HID, 128), scratch(BF16, 256, 128), scratch(BF16, 256, 128),
             scratch(BF16, 256, 128), scratch(BF16, 3, 64, 128),
-            scratch(F32, 64, 128), scratch(F32, 7, 8, 128), scratch(F32, 8, 8, 128),
+            scratch(F32, 8, 16, 128), scratch(F32, 8, 16, 128), scratch(F32, 8, 16, 128),
             scratch(F32, 2, 8, 128), scratch(F32, 4, 8, 128),
-            scratch(F32, 8, 8, 128), scratch(F32, 8, 8, 128),
-            pltpu.SemaphoreType.DMA((4,)),
+            pltpu.SemaphoreType.DMA((9,)),
             pltpu.SemaphoreType.DMA((N_SEMS,)), pltpu.SemaphoreType.DMA((N_SEMS,)),
         ],
         compiler_params=pltpu.CompilerParams(
@@ -457,13 +488,18 @@
         cost_estimate=pl.CostEstimate(
             flops=4 * DIN * HID * COLS, bytes_accessed=4 * 2**20, transcendentals=2 * HID * COLS),
         name="energy_score_step",
-    )(
-        latent, w_in, b_in.reshape(1, HID), output_weight, output_bias.reshape(1, VARS),
-        observed_field, area.reshape(1, COLS),
-    )
+    )(*[pltpu.with_memory_space_constraint(operand, pltpu.HBM) for operand in operands])
+    loss, grad_w_in, grad_b_in, grad_w_out, grad_b_out = pl.pallas_call(
+        deliver,
+        out_shape=results,
+        in_specs=[vmem] * 5,
+        out_specs=(hbm,) * 5,
+        scratch_shapes=[pltpu.SemaphoreType.DMA((5,))],
+        name="deliver",
+    )(*made)
     return (
-        loss.reshape(COLS), grad_w_in, small[0:4].reshape(HID), grad_w_out[:, 0:VARS],
-        small[4, 0:VARS],
+        loss.reshape(COLS), grad_w_in, grad_b_in.reshape(HID), grad_w_out.T,
+        grad_b_out.reshape(VARS),
     )
 
 

time: 65.6 us -> 63.8 us (0.973)
  local copies, waits for them, and re-layouts: 7.03 us -> 2.77 us
  Pallas kernels: 57.6 us -> 60.3 us
    unnamed x16 -> x10, local copies, waits for them, and re-layouts: 5.93 us -> 2.77 us
    pallas_call x1 -> x2, Pallas kernels: 57.6 us -> 60.3 us  [the longest x1 57.9 us: per_device(): pl.pallas_call(lambda *refs: kernel(total_columns, *refs), out_shape=resu...]
where the time goes in v2:
time: 63.8 us; the launch traced here: 63.7 us
  Pallas kernels  60.3 us (95%)
  local copies, waits for them, and re-layouts  2.77 us (4%)
  between operations  0.65 us (1%)
    pallas_call x1, Pallas kernels, per_device(): pl.pallas_call(lambda *refs: kernel(total_columns, *refs), out_shape=resu...  57.9 us
    unnamed x10, local copies, waits for them, and re-layouts  2.77 us
    pallas_call x1, Pallas kernels, per_device(): pl.pallas_call(deliver, out_shape=results, in_specs=[vmem] * 5, out_specs...  2.31 us

profile of v2, /device:TPU:1, one launch (start us, length us, event | category | flops | bytes accessed | tf_op | source)
XLA Modules:
  0.0 63.7 jit_solution(10456287834993212136)
XLA Ops:
  0.6 57.9 %energy_score_step.1 = (f32[1,512]{1,0:T(1,128)S(1)}, bf16[1024,512]{1,0:T(8,128)(2,1)S(1)}, f32[1,512]{1,0:T(1,128)S(1)}, f32[83,512]{1,0:T(8,128)S(1)}, f32[1,83]{1,0:T(1,128)S(1)}) custom-call(bf16[1,1024,512]{2,1,0:T(8,128)(2,1)} %refs_0_.1, bf16[1024,512]{1,0:T(8,128)(2,1)} %refs_1_.1, f32[1,512]{1,0:T(1,128)} %bitcast.10, bf16[83,512]{1,0:T(8,128)(2,1)} %bitcast.9, ...), custom_call_target="tpu_custom_call" | custom-call | flops 1073741824 | bytes 4194304 | tf_op jit(solution)/shard_map/energy_score_step/pallas_call | solution.py:458
  58.6 0.0 copy-start
  58.6 1.0 %copy-done = bf16[1024,512]{1,0:T(8,128)(2,1)} copy-done((bf16[1024,512]{1,0:T(8,128)(2,1)}, bf16[1024,512]{1,0:T(8,128)(2,1)S(1)}, u32[]{:S(2)}) %copy-start) | copy-done | bytes 1048600
  59.6 0.0 copy-start.1
  59.6 0.7 %copy-done.1 = f32[83,512]{1,0:T(8,128)} copy-done((f32[83,512]{1,0:T(8,128)}, f32[83,512]{1,0:T(8,128)S(1)}, u32[]{:S(2)}) %copy-start.1) | copy-done | bytes 170008
  60.2 0.0 copy-start.4
  60.2 0.5 copy-done.4
  60.8 0.0 copy-start.2
  60.8 0.0 copy-start.3
  60.8 0.6 copy-done.2
  61.4 0.0 copy-done.3
  61.4 2.3 %deliver.1 = (f32[1,512]{1,0:T(1,128)}, bf16[1024,512]{1,0:T(8,128)(2,1)}, f32[1,512]{1,0:T(1,128)}, f32[83,512]{1,0:T(8,128)}, f32[1,83]{1,0:T(1,128)}) custom-call(f32[1,512]{1,0:T(1,128)} %copy-done.2, bf16[1024,512]{1,0:T(8,128)(2,1)} %copy-done, f32[1,512]{1,0:T(1,128)} %copy-done.3, f32[83,512]{1,0:T(8,128)} %copy-done.1, f32[1,83]{1,0:T(1,128)} %copy-done.4), custom_call_target="tpu_custom_call" | custom-call | tf_op jit(solution)/shard_map/deliver/pallas_call | solution.py:492
Async XLA Ops:
  58.6 1.0 %copy-start = (bf16[1024,512]{1,0:T(8,128)(2,1)}, bf16[1024,512]{1,0:T(8,128)(2,1)S(1)}, u32[]{:S(2)}) copy-start(bf16[1024,512]{1,0:T(8,128)(2,1)S(1)} %get-tuple-element.16.refs_1_) | copy-start | bytes 3145732
  59.6 0.7 %copy-start.1 = (f32[83,512]{1,0:T(8,128)}, f32[83,512]{1,0:T(8,128)S(1)}, u32[]{:S(2)}) copy-start(f32[83,512]{1,0:T(8,128)S(1)} %get-tuple-element.18.refs_3_) | copy-start | bytes 509956
  60.2 0.5 copy-start.4
  60.8 0.6 copy-start.2
  60.8 0.6 copy-start.3

commit v3 on v2

--- a/solution.py
+++ b/solution.py
@@ -20,7 +20,7 @@
 NX, NU = 4, 8
 FAR4 = (2, 1, 3)
 FAR8 = (4, 3, 5, 2, 6, 1, 7)
-N_SEMS = 160
+N_SENDS, N_RECEIVES = 24, 34
 
 
 def dot(a, b):
@@ -49,24 +49,23 @@
     local_sems, send_sems, recv_sems,
 ):
     member, grid = lax.axis_index("member"), lax.axis_index("grid")
-    c, zlo = member % 2, member // 2
-    a, b = zlo // 2, zlo % 2
-    zhi, y, x = grid % 2, (grid // 2) % 8, grid // 16
+    c, zlo = member & 1, member >> 1
+    a, b = zlo >> 1, zlo & 1
+    zhi, y, x = grid & 1, (grid >> 1) & 7, grid >> 4
     z = zhi * 4 + zlo
-    u = y * (1 - c) + z * c
-    v = z * (1 - c) + y * c
-
-    def device(x, y, z, c):
-        return ((z % 4) * 2 + c, (x * 8 + y) * 2 + z // 4)
-
-    def to_x(k):
-        return device((x + k) % 4, y, z, c)
-
-    def to_u(k):
-        return device(x, (y + k * (1 - c)) % 8, (z + k * c) % 8, c)
-
-    def to_v(k):
-        return device(x, (y + k * c) % 8, (z + k * (1 - c)) % 8, c)
+    on_y = 1 - c
+    u = y * on_y + z * c
+    v = z * on_y + y * c
+
+    def device(x, y, z):
+        return ((z & 3) * 2 + c, (x * 8 + y) * 2 + (z >> 2))
+
+    x_at = [(x + k) & 3 for k in range(4)]
+    u_at = [(u + k) & 7 for k in range(8)]
+    v_at = [(v + k) & 7 for k in range(8)]
+    to_x = [(member, (x_at[k] * 8 + y) * 2 + zhi) for k in range(4)]
+    to_u = [device(x, u_at[k] * on_y + y * c, z * on_y + u_at[k] * c) for k in range(8)]
+    to_v = [device(x, y * on_y + v_at[k] * c, v_at[k] * on_y + z * c) for k in range(8)]
 
     sibling = (zlo * 2 + 1 - c, grid)
 
@@ -79,31 +78,44 @@
 
     rels = [(ra, rb, rc) for ra in (1, 0) for rb in (1, 0) for rc in (1, 0)][:-1]
 
-    started, fences = [], [0, 0]
+    there = {rel: member_of(rel) for rel in rels}
+
+    groups, fences, received = [], [0, 0], [0]
+
+    class Group:
+        def __init__(self, size, apart=0):
+            self.size, self.index = size, len(groups)
+            self.first, self.apart, self.count = received[0], apart, 0
+            received[0] += max(apart, 1)
+            groups.append(self)
+
+        def copy(self, src, dst, to, number=0):
+            return pltpu.make_async_remote_copy(
+                src_ref=src, dst_ref=dst, send_sem=send_sems.at[self.index],
+                recv_sem=recv_sems.at[self.first + number], device_id=to, device_id_type=MESH,
+            )
+
+        def send(self, src, dst, to):
+            copy = self.copy(src, dst, to, self.count if self.apart else 0)
+            self.count += 1
+            copy.start()
+            return copy
+
+        def arrived(self):
+            self.copy(self.size, self.size, sibling).wait_recv()
+
+        def left(self):
+            self.copy(self.size, self.size, sibling).wait_send()
 
     def drain():
-        for copy in started[fences[-2]:fences[-1]]:
-            copy.wait_send()
-        fences.append(len(started))
-
-    def send(src, dst, to):
-        i = len(started)
-        copy = pltpu.make_async_remote_copy(
-            src_ref=src, dst_ref=dst, send_sem=send_sems.at[i], recv_sem=recv_sems.at[i],
-            device_id=to, device_id_type=MESH,
-        )
-        copy.start()
-        started.append(copy)
-        return copy
-
-    def arrived(copies):
-        for copy in copies:
-            copy.wait_recv()
+        for group in groups[fences[-2]:fences[-1]]:
+            group.left()
+        fences.append(len(groups))
 
     barrier = pltpu.get_barrier_semaphore()
     partners = (
-        [(member_of(rel), grid) for rel in rels]
-        + [to_x(k) for k in FAR4] + [to_u(k) for k in FAR8] + [to_v(k) for k in FAR8]
+        [to_u[k] for k in FAR8] + [to_v[k] for k in FAR8]
+        + [(there[rel], grid) for rel in rels] + [to_x[k] for k in FAR4]
     )
     for partner in partners:
         pl.semaphore_signal(barrier, inc=1, device_id=partner, device_id_type=MESH)
@@ -149,7 +161,7 @@
     for copy in load_w:
         copy.wait()
 
-    f_copies = []
+    f_group = Group(f_recv.at[pl.ds(0, 7)])
     for i, h in enumerate(halves):
         cols = pl.ds(pl.multiple_of(h * 256, 256), 256)
         load_l[i].wait()
@@ -176,7 +188,7 @@
         for rel in rels:
             if rel[0] == 1 - i:
                 src = f_send.at[i, flip(b, rel[1]), flip(c, rel[2])]
-                f_copies.append(send(src, f_recv.at[member], (member_of(rel), grid)))
+                f_group.send(src, f_recv.at[member], (there[rel], grid))
     f_recv[pl.ds(member, 1)] = f_send[1, pl.ds(b, 1), pl.ds(c, 1)].reshape(1, FOLD, 128)
 
     def derive(r, _):
@@ -209,7 +221,7 @@
         inverse = lax.rsqrt(square)
         return square * inverse, inverse
 
-    arrived(f_copies)
+    f_group.arrived()
     fields = [f_recv[i].astype(F32) for i in range(8)]
     grads = []
     true_total = jnp.zeros((1, 128), F32)
@@ -229,18 +241,18 @@
             grads[n] = grads[n] + pull
     for m in range(8):
         g_send[m] = grads[m].astype(BF16)
-    g_copies = []
+    g_group = Group(g_recv.at[pl.ds(0, 7)])
     for rel in rels:
-        there = member_of(rel)
-        g_copies.append(send(g_send.at[there], g_recv.at[member], (there, grid)))
+        g_group.send(g_send.at[there[rel]], g_recv.at[member], (there[rel], grid))
     g_recv[pl.ds(member, 1)] = g_send[pl.ds(member, 1)]
     loss = true_total * (1.0 / 8) - pair_total * (1.0 / 128)
     loss_recv[pl.ds(member, 1)] = jnp.broadcast_to(loss, (1, 8, 128))
-    loss_copies = [
-        send(loss_recv.at[member], loss_recv.at[member], (member_of(rel), grid)) for rel in rels]
-
-    drain()
-    arrived(g_copies)
+    loss_group = Group(loss_recv.at[pl.ds(0, 7)])
+    for rel in rels:
+        loss_group.send(loss_recv.at[member], loss_recv.at[member], (there[rel], grid))
+
+    drain()
+    g_group.arrived()
     for t in range(4):
         left, right = g_recv[2 * t].astype(F32), g_recv[2 * t + 1].astype(F32)
         cols = pl.ds(128 * t, 128)
@@ -254,14 +266,15 @@
 
     lax.fori_loop(0, HID // 128, grad_hidden, 0)
 
-    sib_copies = [None, None]
+    sib_groups = [Group(sib_recv.at[q]) for q in range(2)]
     for q in (1, 0):
         rows = pl.ds(pl.multiple_of((1 - c) * 512 + q * 256, 256), 256)
         sib_send[q] = dot_nt(lat[rows, :], gp[...]).astype(BF16)
-        sib_copies[q] = send(sib_send.at[q], sib_recv.at[q], sibling)
+        sib_groups[q].send(sib_send.at[q], sib_recv.at[q], sibling)
     wo_part[...] = dot_nt(hidden[...], gl[...])
     wo_send[...] = wo_part[pl.ds(pl.multiple_of((1 - c) * 256, 256), 256), :].astype(BF16)
-    wo_copy = send(wo_send, wo_recv, sibling)
+    wo_group = Group(wo_recv)
+    wo_group.send(wo_send, wo_recv, sibling)
     ones = jnp.ones((16, COLS), BF16)
     sum_in = dot_nt(ones, gp[...])[0:1]
     sum_out = dot_nt(ones, gl[...])[0:1]
@@ -270,7 +283,8 @@
     for i in range(4):
         tile = jnp.where(rows8 == i, sum_in[:, 128 * i:128 * i + 128], tile)
     sm_c[pl.ds(c, 1)] = tile.reshape(1, 8, 128)
-    smc_copy = send(sm_c.at[c], sm_c.at[c], sibling)
+    smc_group = Group(sm_c.at[0])
+    smc_group.send(sm_c.at[c], sm_c.at[c], sibling)
 
     x_cols = pl.ds(pl.multiple_of(x * 128, 128), 128)
     u_rows = pl.ds(pl.multiple_of(u * 32, 32), 32)
@@ -280,80 +294,88 @@
         own[q] = dot_nt(lat[rows, :], gp[...])
 
     def merge(q):
-        sib_copies[q].wait_recv()
+        sib_groups[q].arrived()
         part[q] = (own[q] + sib_recv[q].astype(F32)).astype(BF16)
 
     own_half(1)
     merge(1)
-    u1_copies = []
-    for k in FAR8:
-        rows = pl.ds(pl.multiple_of((u + k) % 8 * 32, 32), 32)
-        u1_copies.append(send(part.at[1, rows], u1_recv.at[k - 1], to_u(k)))
+    u1_group = Group(u1_recv)
+    for k in FAR8:
+        rows = pl.ds(pl.multiple_of(u_at[k] * 32, 32), 32)
+        u1_group.send(part.at[1, rows], u1_recv.at[k - 1], to_u[k])
     own_half(0)
     merge(0)
-    x0_copies = []
+    x0_group = Group(x0_recv)
     for k in FAR4:
-        cols = pl.ds(pl.multiple_of((x + k) % 4 * 128, 128), 128)
-        x0_copies.append(send(part.at[0, :, cols], x0_recv.at[k - 1], to_x(k)))
-    wo_copy.wait_recv()
+        cols = pl.ds(pl.multiple_of(x_at[k] * 128, 128), 128)
+        x0_group.send(part.at[0, :, cols], x0_recv.at[k - 1], to_x[k])
+    wo_group.arrived()
     wo_rs[...] = (
         wo_part[pl.ds(pl.multiple_of(c * 256, 256), 256), :] + wo_recv[...].astype(F32)).astype(BF16)
-    wox_copies = []
+    wox_group = Group(wox_recv)
     for k in FAR4:
-        rows = pl.ds(pl.multiple_of((x + k) % 4 * 64, 64), 64)
-        wox_copies.append(send(wo_rs.at[rows], wox_recv.at[k - 1], to_x(k)))
-    smc_copy.wait_recv()
+        rows = pl.ds(pl.multiple_of(x_at[k] * 64, 64), 64)
+        wox_group.send(wo_rs.at[rows], wox_recv.at[k - 1], to_x[k])
+    smc_group.arrived()
     sm_x[pl.ds(x, 1)] = (sm_c[0] + sm_c[1]).reshape(1, 8, 128)
-    smx_copies = [send(sm_x.at[x], sm_x.at[x], to_x(k)) for k in FAR4]
-
-    drain()
-    arrived(x0_copies)
+    smx_group = Group(sm_x.at[pl.ds(0, 3)])
+    for k in FAR4:
+        smx_group.send(sm_x.at[x], sm_x.at[x], to_x[k])
+
+    drain()
+    x0_group.arrived()
     total = part[0, :, x_cols].astype(F32)
     for k in range(3):
         total = total + x0_recv[k].astype(F32)
     s0[...] = total.astype(BF16)
-    u0_copies = []
-    for k in FAR8:
-        rows = pl.ds(pl.multiple_of((u + k) % 8 * 32, 32), 32)
-        u0_copies.append(send(s0.at[rows], u0_recv.at[k - 1], to_u(k)))
-    arrived(wox_copies)
+    u0_group = Group(u0_recv)
+    for k in FAR8:
+        rows = pl.ds(pl.multiple_of(u_at[k] * 32, 32), 32)
+        u0_group.send(s0.at[rows], u0_recv.at[k - 1], to_u[k])
+    wox_group.arrived()
     total = wo_rs[pl.ds(pl.multiple_of(x * 64, 64), 64), :].astype(F32)
     for k in range(3):
         total = total + wox_recv[k].astype(F32)
-    arrived(smx_copies)
+    smx_group.arrived()
     small = sm_x[0] + sm_x[1] + sm_x[2] + sm_x[3]
     for j in range(8):
         wou_src[j, 0:8] = total[8 * j:8 * j + 8]
         wou_src[j, 8:16] = small
     wou_recv[pl.ds(u, 1)] = wou_src[pl.ds(u, 1)]
-    wou_copies = [send(wou_src.at[(u + k) % 8], wou_recv.at[u], to_u(k)) for k in FAR8]
-    arrived(u1_copies)
+    wou_group = Group(wou_recv.at[pl.ds(0, 7)])
+    for k in FAR8:
+        wou_group.send(wou_src.at[u_at[k]], wou_recv.at[u], to_u[k])
+    u1_group.arrived()
     total = part[1, u_rows, :].astype(F32)
     for k in range(7):
         total = total + u1_recv[k].astype(F32)
     s1[...] = total.astype(BF16)
-    x1_copies = []
+    x1_group = Group(x1_recv)
     for k in FAR4:
-        cols = pl.ds(pl.multiple_of((x + k) % 4 * 128, 128), 128)
-        x1_copies.append(send(s1.at[:, cols], x1_recv.at[k - 1], to_x(k)))
-
-    arrived(x1_copies)
+        cols = pl.ds(pl.multiple_of(x_at[k] * 128, 128), 128)
+        x1_group.send(s1.at[:, cols], x1_recv.at[k - 1], to_x[k])
+
+    x1_group.arrived()
     total = s1[:, x_cols].astype(F32)
     for k in range(3):
         total = total + x1_recv[k].astype(F32)
     v_recv[v, 1] = total.astype(BF16)
-    arrived(u0_copies)
+    u0_group.arrived()
     total = s0[u_rows, :].astype(F32)
     for k in range(7):
         total = total + u0_recv[k].astype(F32)
     v_recv[v, 0] = total.astype(BF16)
-    v_copies = [send(v_recv.at[v], v_recv.at[v], to_v(k)) for k in FAR8]
-    arrived(wou_copies)
+    v_group = Group(v_recv.at[pl.ds(0, 7)])
+    for k in FAR8:
+        v_group.send(v_recv.at[v], v_recv.at[v], to_v[k])
+    wou_group.arrived()
     total = wou_recv[0]
     for k in range(1, 8):
         total = total + wou_recv[k]
     wov_recv[pl.ds(v, 1)] = total.reshape(1, 16, 128)
-    wov_copies = [send(wov_recv.at[v], wov_recv.at[v], to_v(k)) for k in FAR8]
+    wov_group = Group(wov_recv.at[pl.ds(0, 7)])
+    for k in FAR8:
+        wov_group.send(wov_recv.at[v], wov_recv.at[v], to_v[k])
     drain()
 
     base = c * 512
@@ -361,7 +383,7 @@
     def block(q, rows_at, rows, cols):
         return gw_ref.at[pl.ds(pl.multiple_of(base + q * 256 + rows_at, 32), rows), cols]
 
-    arrived(v_copies)
+    v_group.arrived()
     total = v_recv[0].astype(F32)
     for k in range(1, 8):
         total = total + v_recv[k].astype(F32)
@@ -370,58 +392,70 @@
     spot1[...] = total[1]
     spot0 = block(0, u * 32, 32, x_cols)
     spot0[...] = total[0]
-    u0_copies = [send(spot0, spot0, to_u(k)) for k in FAR8]
-    x1_copies = [send(spot1, spot1, to_x(k)) for k in FAR4]
-    arrived(wov_copies)
+    u0_group = Group(u0_recv)
+    for k in FAR8:
+        u0_group.send(spot0, spot0, to_u[k])
+    x1_group = Group(x1_recv)
+    for k in FAR4:
+        x1_group.send(spot1, spot1, to_x[k])
+    wov_group.arrived()
     total = wov_recv[0]
     for k in range(1, 8):
         total = total + wov_recv[k]
     spot = gwo.at[pl.ds(pl.multiple_of(c * 256 + x * 64 + u * 8, 8), 8)]
     spot[...] = total[0:8]
-    wou_copies = [send(spot, spot, to_u(k)) for k in FAR8]
+    wou_group = Group(loss_recv.at[pl.ds(0, 7)])
+    for k in FAR8:
+        wou_group.send(spot, spot, to_u[k])
     for i in range(4):
         gbin_ref[:, 128 * i:128 * i + 128] = total[8 + i:9 + i]
     gbo_ref[...] = total[12:13, 0:VARS]
     drain()
 
-    arrived(x1_copies)
+    x1_group.arrived()
     spot = block(1, u * 32, 32, pl.ds(0, 512))
-    u1_copies = [send(spot, spot, to_u(k)) for k in FAR8]
-    last = [send(spot, spot, sibling)]
-    arrived(u0_copies)
+    u1_group = Group(u1_recv, apart=7)
+    u1_copies = [u1_group.send(spot, spot, to_u[k]) for k in FAR8]
+    last = Group(part)
+    last.send(spot, spot, sibling)
+    u0_group.arrived()
     spot = block(0, 0, 256, x_cols)
-    x0_copies = [send(spot, spot, to_x(k)) for k in FAR4]
-    last.append(send(spot, spot, sibling))
-    arrived(wou_copies)
+    x0_group = Group(x0_recv, apart=3)
+    x0_copies = [x0_group.send(spot, spot, to_x[k]) for k in FAR4]
+    last.send(spot, spot, sibling)
+    wou_group.arrived()
     spot = gwo.at[pl.ds(pl.multiple_of(c * 256 + x * 64, 64), 64)]
-    wox_copies = [send(spot, spot, to_x(k)) for k in FAR4]
-    last_wo = [send(spot, spot, sibling)]
-
-    drain()
-    arrived(loss_copies)
+    wox_group = Group(gwo.at[pl.ds(0, 192)], apart=3)
+    wox_copies = [wox_group.send(spot, spot, to_x[k]) for k in FAR4]
+    last_wo = Group(gwo.at[pl.ds(0, 256)])
+    last_wo.send(spot, spot, sibling)
+
+    drain()
+    loss_group.arrived()
     for t in range(4):
         loss_ref[:, 128 * t:128 * t + 128] = jnp.where(
             low_row, loss_recv[2 * t, 0:1, :], loss_recv[2 * t + 1, 0:1, :])
 
     for k, copy in reversed(list(zip(FAR4, wox_copies))):
         copy.wait_recv()
-        spot = gwo.at[pl.ds(pl.multiple_of(c * 256 + (x + 4 - k) % 4 * 64, 64), 64)]
-        last_wo.append(send(spot, spot, sibling))
+        spot = gwo.at[pl.ds(pl.multiple_of(c * 256 + x_at[4 - k] * 64, 64), 64)]
+        last_wo.send(spot, spot, sibling)
     near_u = [(k, copy, u1_copies) for k, copy in zip(FAR8, u1_copies)][::-1]
     near_x = [(k, copy, x0_copies) for k, copy in zip(FAR4, x0_copies)][::-1]
     for k, copy, group in near_u[:4] + near_x[:2] + near_u[4:] + near_x[2:]:
         copy.wait_recv()
         if group is x0_copies:
-            cols = pl.ds(pl.multiple_of((x + 4 - k) % 4 * 128, 128), 128)
+            cols = pl.ds(pl.multiple_of(x_at[4 - k] * 128, 128), 128)
             spot = block(0, 0, 256, cols)
         else:
-            spot = block(1, (u + 8 - k) % 8 * 32, 32, pl.ds(0, 512))
-        last.append(send(spot, spot, sibling))
-    arrived(last_wo)
+            spot = block(1, u_at[8 - k] * 32, 32, pl.ds(0, 512))
+        last.send(spot, spot, sibling)
+    last_wo.arrived()
     gwo_ref[...] = jnp.transpose(gwo[...])[0:VARS]
-    arrived(last)
-    drain()
-    drain()
+    last.arrived()
+    drain()
+    drain()
+    assert len(groups) == N_SENDS and received[0] == N_RECEIVES
 
 
 def deliver(*refs):
@@ -481,7 +515,7 @@
             scratch(F32, 8, 16, 128), scratch(F32, 8, 16, 128), scratch(F32, 8, 16, 128),
             scratch(F32, 2, 8, 128), scratch(F32, 4, 8, 128),
             pltpu.SemaphoreType.DMA((9,)),
-            pltpu.SemaphoreType.DMA((N_SEMS,)), pltpu.SemaphoreType.DMA((N_SEMS,)),
+            pltpu.SemaphoreType.DMA((N_SENDS,)), pltpu.SemaphoreType.DMA((N_RECEIVES,)),
         ],
         compiler_params=pltpu.CompilerParams(
             collective_id=0, has_side_effects=True, vmem_limit_bytes=40 * 2**20),
@@ -495,6 +529,7 @@
         in_specs=[vmem] * 5,
         out_specs=(hbm,) * 5,
         scratch_shapes=[pltpu.SemaphoreType.DMA((5,))],
+        compiler_params=pltpu.CompilerParams(vmem_limit_bytes=4 * 2**20),
         name="deliver",
     )(*made)
     return (

time: 63.8 us -> 57.1 us (0.89)
  Pallas kernels: 60.3 us -> 56.3 us
  local copies, waits for them, and re-layouts: 2.77 us -> 0 us
    unnamed x10 -> x0, local copies, waits for them, and re-layouts: 2.77 us -> none
    pallas_call x1, Pallas kernels: 57.9 us -> 55.3 us  [per_device(): pl.pallas_call(lambda *refs: kernel(total_columns, *refs), out_shape=resu...]
    pallas_call x1, Pallas kernels: 2.31 us -> 1.07 us  [per_device(): pl.pallas_call(deliver, out_shape=results, in_specs=[vmem] * 5, out_specs...]
where the time goes in v3:
time: 57.1 us; the launch traced here: 57 us
  Pallas kernels  56.3 us (99%)
  between operations  0.64 us (1%)
    pallas_call x1, Pallas kernels, per_device(): pl.pallas_call(lambda *refs: kernel(total_columns, *refs), out_shape=resu...  55.3 us

profile of v3, /device:TPU:1, one launch (start us, length us, event | category | flops | bytes accessed | tf_op | source)
XLA Modules:
  0.0 57.0 jit_solution(5739278060151985632)
XLA Ops:
  0.6 55.3 %energy_score_step.1 = (f32[1,512]{1,0:T(1,128)S(1)}, bf16[1024,512]{1,0:T(8,128)(2,1)S(1)}, f32[1,512]{1,0:T(1,128)S(1)}, f32[83,512]{1,0:T(8,128)S(1)}, f32[1,83]{1,0:T(1,128)S(1)}) custom-call(bf16[1,1024,512]{2,1,0:T(8,128)(2,1)} %refs_0_.1, bf16[1024,512]{1,0:T(8,128)(2,1)} %refs_1_.1, f32[1,512]{1,0:T(1,128)} %bitcast.10, bf16[83,512]{1,0:T(8,128)(2,1)} %bitcast.9, ...), custom_call_target="tpu_custom_call" | custom-call | flops 1073741824 | bytes 4194304 | tf_op jit(solution)/shard_map/energy_score_step/pallas_call | solution.py:492
  55.9 1.1 %deliver.1 = (f32[1,512]{1,0:T(1,128)}, bf16[1024,512]{1,0:T(8,128)(2,1)}, f32[1,512]{1,0:T(1,128)}, f32[83,512]{1,0:T(8,128)}, f32[1,83]{1,0:T(1,128)}) custom-call(f32[1,512]{1,0:T(1,128)S(1)} %get-tuple-element.15.refs_0_, bf16[1024,512]{1,0:T(8,128)(2,1)S(1)} %get-tuple-element.16.refs_1_, f32[1,512]{1,0:T(1,128)S(1)} %get-tuple-element.17.refs_2_, ...), custom_call_target="tpu_custom_call" | custom-call | tf_op jit(solution)/shard_map/deliver/pallas_call | solution.py:526

commit v4 on v3

--- a/solution.py
+++ b/solution.py
@@ -39,7 +39,7 @@
     total_columns,
     lat_hbm, win_hbm, bin_hbm, wo_hbm, bo_hbm, obs_hbm, area_hbm,
     loss_ref, gw_ref, gbin_ref, gwo_ref, gbo_ref,
-    bin_ref, wo_ref, bo_ref, obs_ref, area_ref, gwo,
+    bin_ref, wo_ref, bo_ref, obs_ref, area_ref, gwo, gwo_low,
     lat, win, bias, pre, dgelu, hidden, wop, wop_t, row, obs_pad,
     f_send, f_recv, g_send, g_recv, loss_recv, gl, gp,
     sib_send, sib_recv, own, part,
@@ -111,14 +111,6 @@
         for group in groups[fences[-2]:fences[-1]]:
             group.left()
         fences.append(len(groups))
-
-    barrier = pltpu.get_barrier_semaphore()
-    partners = (
-        [to_u[k] for k in FAR8] + [to_v[k] for k in FAR8]
-        + [(there[rel], grid) for rel in rels] + [to_x[k] for k in FAR4]
-    )
-    for partner in partners:
-        pl.semaphore_signal(barrier, inc=1, device_id=partner, device_id_type=MESH)
 
     halves = [1 - a, a]
     load_w = [
@@ -138,7 +130,20 @@
             (bin_hbm, bin_ref), (wo_hbm, wo_ref), (bo_hbm, bo_ref),
             (obs_hbm, obs_ref), (area_hbm, area_ref)))
     ]
-    for copy in load_w + load_small[:3] + load_l + load_small[3:]:
+    for copy in load_w + load_l[:1] + load_small[:3]:
+        copy.start()
+
+    barrier = pltpu.get_barrier_semaphore()
+    far, near = rels[:4], rels[4:]
+    partners = (
+        [way[k] for k in (4, 3, 5) for way in (to_u, to_v)] + [(there[rel], grid) for rel in far]
+        + [way[k] for k in (2, 6) for way in (to_u, to_v)] + [to_x[2]]
+        + [(there[rel], grid) for rel in near]
+        + [way[k] for k in (1, 7) for way in (to_u, to_v)] + [to_x[1], to_x[3]]
+    )
+    for partner in partners:
+        pl.semaphore_signal(barrier, inc=1, device_id=partner, device_id_type=MESH)
+    for copy in load_l[1:] + load_small[3:]:
         copy.start()
 
     wop_t[...] = jnp.zeros_like(wop_t)
@@ -267,7 +272,7 @@
     lax.fori_loop(0, HID // 128, grad_hidden, 0)
 
     sib_groups = [Group(sib_recv.at[q]) for q in range(2)]
-    for q in (1, 0):
+    for q in range(2):
         rows = pl.ds(pl.multiple_of((1 - c) * 512 + q * 256, 256), 256)
         sib_send[q] = dot_nt(lat[rows, :], gp[...]).astype(BF16)
         sib_groups[q].send(sib_send.at[q], sib_recv.at[q], sibling)
@@ -297,18 +302,18 @@
         sib_groups[q].arrived()
         part[q] = (own[q] + sib_recv[q].astype(F32)).astype(BF16)
 
+    own_half(0)
     own_half(1)
-    merge(1)
-    u1_group = Group(u1_recv)
-    for k in FAR8:
-        rows = pl.ds(pl.multiple_of(u_at[k] * 32, 32), 32)
-        u1_group.send(part.at[1, rows], u1_recv.at[k - 1], to_u[k])
-    own_half(0)
     merge(0)
     x0_group = Group(x0_recv)
     for k in FAR4:
         cols = pl.ds(pl.multiple_of(x_at[k] * 128, 128), 128)
         x0_group.send(part.at[0, :, cols], x0_recv.at[k - 1], to_x[k])
+    merge(1)
+    u1_group = Group(u1_recv)
+    for k in FAR8:
+        rows = pl.ds(pl.multiple_of(u_at[k] * 32, 32), 32)
+        u1_group.send(part.at[1, rows], u1_recv.at[k - 1], to_u[k])
     wo_group.arrived()
     wo_rs[...] = (
         wo_part[pl.ds(pl.multiple_of(c * 256, 256), 256), :] + wo_recv[...].astype(F32)).astype(BF16)
@@ -424,10 +429,12 @@
     x0_copies = [x0_group.send(spot, spot, to_x[k]) for k in FAR4]
     last.send(spot, spot, sibling)
     wou_group.arrived()
-    spot = gwo.at[pl.ds(pl.multiple_of(c * 256 + x * 64, 64), 64)]
-    wox_group = Group(gwo.at[pl.ds(0, 192)], apart=3)
+    rows = pl.ds(pl.multiple_of(c * 256 + x * 64, 64), 64)
+    spot = gwo_low.at[rows]
+    spot[...] = gwo[rows].astype(BF16)
+    wox_group = Group(wox_recv, apart=3)
     wox_copies = [wox_group.send(spot, spot, to_x[k]) for k in FAR4]
-    last_wo = Group(gwo.at[pl.ds(0, 256)])
+    last_wo = Group(wo_recv)
     last_wo.send(spot, spot, sibling)
 
     drain()
@@ -438,7 +445,7 @@
 
     for k, copy in reversed(list(zip(FAR4, wox_copies))):
         copy.wait_recv()
-        spot = gwo.at[pl.ds(pl.multiple_of(c * 256 + x_at[4 - k] * 64, 64), 64)]
+        spot = gwo_low.at[pl.ds(pl.multiple_of(c * 256 + x_at[4 - k] * 64, 64), 64)]
         last_wo.send(spot, spot, sibling)
     near_u = [(k, copy, u1_copies) for k, copy in zip(FAR8, u1_copies)][::-1]
     near_x = [(k, copy, x0_copies) for k, copy in zip(FAR4, x0_copies)][::-1]
@@ -451,7 +458,7 @@
             spot = block(1, u_at[8 - k] * 32, 32, pl.ds(0, 512))
         last.send(spot, spot, sibling)
     last_wo.arrived()
-    gwo_ref[...] = jnp.transpose(gwo[...])[0:VARS]
+    gwo_ref[...] = jnp.transpose(gwo_low[...].astype(F32))[0:VARS]
     last.arrived()
     drain()
     drain()
@@ -497,6 +504,7 @@
         scratch_shapes=[
             scratch(F32, 1, HID), scratch(BF16, VARS, HID), scratch(F32, 1, VARS),
             scratch(F32, VARS, COLS), scratch(F32, 1, COLS), scratch(F32, HID, 128),
+            scratch(BF16, HID, 128),
             scratch(BF16, DIN, COLS), scratch(BF16, DIN, HID),
             scratch(F32, HID, 128), scratch(F32, HID, COLS), scratch(F32, HID, COLS),
             scratch(BF16, HID, COLS), scratch(BF16, HID, 128), scratch(BF16, 128, HID),

time: 57.1 us -> 56.9 us (level)
  no operation moved by 1% of the time
where the time goes in v4:
time: 56.9 us; the launch traced here: 56.8 us
  Pallas kernels  56.1 us (99%)
  between operations  0.64 us (1%)
    pallas_call x1, Pallas kernels, per_device(): pl.pallas_call(lambda *refs: kernel(total_columns, *refs), out_shape=resu...  55.1 us

profile of v4, /device:TPU:1, one launch (start us, length us, event | category | flops | bytes accessed | tf_op | source)
XLA Modules:
  0.0 56.8 jit_solution(328094208368848537)
XLA Ops:
  0.6 55.1 %energy_score_step.1 = (f32[1,512]{1,0:T(1,128)S(1)}, bf16[1024,512]{1,0:T(8,128)(2,1)S(1)}, f32[1,512]{1,0:T(1,128)S(1)}, f32[83,512]{1,0:T(8,128)S(1)}, f32[1,83]{1,0:T(1,128)S(1)}) custom-call(bf16[1,1024,512]{2,1,0:T(8,128)(2,1)} %refs_0_.1, bf16[1024,512]{1,0:T(8,128)(2,1)} %refs_1_.1, f32[1,512]{1,0:T(1,128)} %bitcast.10, bf16[83,512]{1,0:T(8,128)(2,1)} %bitcast.9, ...), custom_call_target="tpu_custom_call" | custom-call | flops 1073741824 | bytes 4194304 | tf_op jit(solution)/shard_map/energy_score_step/pallas_call | solution.py:499
  55.7 1.1 %deliver.1 = (f32[1,512]{1,0:T(1,128)}, bf16[1024,512]{1,0:T(8,128)(2,1)}, f32[1,512]{1,0:T(1,128)}, f32[83,512]{1,0:T(8,128)}, f32[1,83]{1,0:T(1,128)}) custom-call(f32[1,512]{1,0:T(1,128)S(1)} %get-tuple-element.15.refs_0_, bf16[1024,512]{1,0:T(8,128)(2,1)S(1)} %get-tuple-element.16.refs_1_, f32[1,512]{1,0:T(1,128)S(1)} %get-tuple-element.17.refs_2_, ...), custom_call_target="tpu_custom_call" | custom-call | tf_op jit(solution)/shard_map/deliver/pallas_call | solution.py:534

commit v5 on v4

--- a/solution.py
+++ b/solution.py
@@ -20,7 +20,7 @@
 NX, NU = 4, 8
 FAR4 = (2, 1, 3)
 FAR8 = (4, 3, 5, 2, 6, 1, 7)
-N_SENDS, N_RECEIVES = 24, 34
+N_SENDS, N_RECEIVES = 24, 28
 
 
 def dot(a, b):
@@ -67,6 +67,7 @@
     to_u = [device(x, u_at[k] * on_y + y * c, z * on_y + u_at[k] * c) for k in range(8)]
     to_v = [device(x, y * on_y + v_at[k] * c, v_at[k] * on_y + z * c) for k in range(8)]
 
+    to_u_other = [(there_u[0] + 1 - 2 * c, there_u[1]) for there_u in to_u]
     sibling = (zlo * 2 + 1 - c, grid)
 
     def flip(bit, by):
@@ -136,10 +137,11 @@
     barrier = pltpu.get_barrier_semaphore()
     far, near = rels[:4], rels[4:]
     partners = (
-        [way[k] for k in (4, 3, 5) for way in (to_u, to_v)] + [(there[rel], grid) for rel in far]
-        + [way[k] for k in (2, 6) for way in (to_u, to_v)] + [to_x[2]]
+        [way[k] for k in (4, 3, 5) for way in (to_u, to_u_other, to_v)]
+        + [(there[rel], grid) for rel in far]
+        + [way[k] for k in (2, 6) for way in (to_u, to_u_other, to_v)] + [to_x[2]]
         + [(there[rel], grid) for rel in near]
-        + [way[k] for k in (1, 7) for way in (to_u, to_v)] + [to_x[1], to_x[3]]
+        + [way[k] for k in (1, 7) for way in (to_u, to_u_other, to_v)] + [to_x[1], to_x[3]]
     )
     for partner in partners:
         pl.semaphore_signal(barrier, inc=1, device_id=partner, device_id_type=MESH)
@@ -419,9 +421,10 @@
 
     x1_group.arrived()
     spot = block(1, u * 32, 32, pl.ds(0, 512))
-    u1_group = Group(u1_recv, apart=7)
-    u1_copies = [u1_group.send(spot, spot, to_u[k]) for k in FAR8]
-    last = Group(part)
+    u1_group, last = Group(u1_recv), Group(part)
+    for k in FAR8:
+        u1_group.send(spot, spot, to_u[k])
+        last.send(spot, spot, to_u_other[k])
     last.send(spot, spot, sibling)
     u0_group.arrived()
     spot = block(0, 0, 256, x_cols)
@@ -443,22 +446,18 @@
         loss_ref[:, 128 * t:128 * t + 128] = jnp.where(
             low_row, loss_recv[2 * t, 0:1, :], loss_recv[2 * t + 1, 0:1, :])
 
+    for k, copy in reversed(list(zip(FAR4, x0_copies))):
+        copy.wait_recv()
+        cols = pl.ds(pl.multiple_of(x_at[4 - k] * 128, 128), 128)
+        spot = block(0, 0, 256, cols)
+        last.send(spot, spot, sibling)
     for k, copy in reversed(list(zip(FAR4, wox_copies))):
         copy.wait_recv()
         spot = gwo_low.at[pl.ds(pl.multiple_of(c * 256 + x_at[4 - k] * 64, 64), 64)]
         last_wo.send(spot, spot, sibling)
-    near_u = [(k, copy, u1_copies) for k, copy in zip(FAR8, u1_copies)][::-1]
-    near_x = [(k, copy, x0_copies) for k, copy in zip(FAR4, x0_copies)][::-1]
-    for k, copy, group in near_u[:4] + near_x[:2] + near_u[4:] + near_x[2:]:
-        copy.wait_recv()
-        if group is x0_copies:
-            cols = pl.ds(pl.multiple_of(x_at[4 - k] * 128, 128), 128)
-            spot = block(0, 0, 256, cols)
-        else:
-            spot = block(1, u_at[8 - k] * 32, 32, pl.ds(0, 512))
-        last.send(spot, spot, sibling)
     last_wo.arrived()
     gwo_ref[...] = jnp.transpose(gwo_low[...].astype(F32))[0:VARS]
+    u1_group.arrived()
     last.arrived()
     drain()
     drain()

time: 56.9 us -> 56.6 us (level)
  no operation moved by 1% of the time
where the time goes in v5:
time: 56.6 us; the launch traced here: 56.5 us
  Pallas kernels  55.8 us (99%)
  between operations  0.64 us (1%)
    pallas_call x1, Pallas kernels, per_device(): pl.pallas_call(lambda *refs: kernel(total_columns, *refs), out_shape=resu...  54.8 us

profile of v5, /device:TPU:1, one launch (start us, length us, event | category | flops | bytes accessed | tf_op | source)
XLA Modules:
  0.0 56.5 jit_solution(914257355735159875)
XLA Ops:
  0.6 54.8 %energy_score_step.1 = (f32[1,512]{1,0:T(1,128)S(1)}, bf16[1024,512]{1,0:T(8,128)(2,1)S(1)}, f32[1,512]{1,0:T(1,128)S(1)}, f32[83,512]{1,0:T(8,128)S(1)}, f32[1,83]{1,0:T(1,128)S(1)}) custom-call(bf16[1,1024,512]{2,1,0:T(8,128)(2,1)} %refs_0_.1, bf16[1024,512]{1,0:T(8,128)(2,1)} %refs_1_.1, f32[1,512]{1,0:T(1,128)} %bitcast.10, bf16[83,512]{1,0:T(8,128)(2,1)} %bitcast.9, ...), custom_call_target="tpu_custom_call" | custom-call | flops 1073741824 | bytes 4194304 | tf_op jit(solution)/shard_map/energy_score_step/pallas_call | solution.py:498
  55.4 1.1 %deliver.1 = (f32[1,512]{1,0:T(1,128)}, bf16[1024,512]{1,0:T(8,128)(2,1)}, f32[1,512]{1,0:T(1,128)}, f32[83,512]{1,0:T(8,128)}, f32[1,83]{1,0:T(1,128)}) custom-call(f32[1,512]{1,0:T(1,128)S(1)} %get-tuple-element.15.refs_0_, bf16[1024,512]{1,0:T(8,128)(2,1)S(1)} %get-tuple-element.16.refs_1_, f32[1,512]{1,0:T(1,128)S(1)} %get-tuple-element.17.refs_2_, ...), custom_call_target="tpu_custom_call" | custom-call | tf_op jit(solution)/shard_map/deliver/pallas_call | solution.py:533

commit v6 on v5

--- a/solution.py
+++ b/solution.py
@@ -17,10 +17,11 @@
 DIN, HID, VARS = 1024, 512, 83
 COLS = 512
 FOLD = 48
+UNIT = 48
 NX, NU = 4, 8
 FAR4 = (2, 1, 3)
 FAR8 = (4, 3, 5, 2, 6, 1, 7)
-N_SENDS, N_RECEIVES = 24, 28
+N_SENDS, N_RECEIVES = 18, 20
 
 
 def dot(a, b):
@@ -39,13 +40,12 @@
     total_columns,
     lat_hbm, win_hbm, bin_hbm, wo_hbm, bo_hbm, obs_hbm, area_hbm,
     loss_ref, gw_ref, gbin_ref, gwo_ref, gbo_ref,
-    bin_ref, wo_ref, bo_ref, obs_ref, area_ref, gwo, gwo_low,
+    bin_ref, wo_ref, bo_ref, obs_ref, area_ref,
     lat, win, bias, pre, dgelu, hidden, wop, wop_t, row, obs_pad,
     f_send, f_recv, g_send, g_recv, loss_recv, gl, gp,
-    sib_send, sib_recv, own, part,
-    x0_recv, s0, u0_recv, u1_recv, s1, x1_recv, v_recv,
-    wo_part, wo_send, wo_recv, wo_rs, wox_recv, wou_src, wou_recv, wov_recv,
-    sm_c, sm_x,
+    sib_send, sib_recv, own, wo_part, wo_send, wo_recv, sm_c,
+    part0, x0_recv, s0, u0_recv, part1, u1_recv, s1, x1_recv, v_recv,
+    gather, gather_other,
     local_sems, send_sems, recv_sems,
 ):
     member, grid = lax.axis_index("member"), lax.axis_index("grid")
@@ -266,6 +266,11 @@
         gl[0:FOLD, cols] = jnp.where(low_lane, left, swap(right)).astype(BF16)
         gl[FOLD:2 * FOLD, cols] = jnp.where(low_lane, swap(left), right).astype(BF16)
 
+    wo_part[...] = dot_nt(gl[...], hidden[...])
+    wo_send[...] = wo_part[:, pl.ds(pl.multiple_of((1 - c) * 256, 256), 256)].astype(BF16)
+    wo_group = Group(wo_recv)
+    wo_group.send(wo_send, wo_recv, sibling)
+
     def grad_hidden(r, _):
         rows = pl.ds(pl.multiple_of(r * 128, 128), 128)
         gp[rows, :] = (dot(wop[rows, :], gl[...]) * dgelu[rows, :]).astype(BF16)
@@ -274,14 +279,21 @@
     lax.fori_loop(0, HID // 128, grad_hidden, 0)
 
     sib_groups = [Group(sib_recv.at[q]) for q in range(2)]
-    for q in range(2):
+
+    def other_half(q):
         rows = pl.ds(pl.multiple_of((1 - c) * 512 + q * 256, 256), 256)
         sib_send[q] = dot_nt(lat[rows, :], gp[...]).astype(BF16)
         sib_groups[q].send(sib_send.at[q], sib_recv.at[q], sibling)
-    wo_part[...] = dot_nt(hidden[...], gl[...])
-    wo_send[...] = wo_part[pl.ds(pl.multiple_of((1 - c) * 256, 256), 256), :].astype(BF16)
-    wo_group = Group(wo_recv)
-    wo_group.send(wo_send, wo_recv, sibling)
+
+    def own_half(q):
+        rows = pl.ds(pl.multiple_of(c * 512 + q * 256, 256), 256)
+        own[q] = dot_nt(lat[rows, :], gp[...])
+
+    def merged(q):
+        sib_groups[q].arrived()
+        return (own[q] + sib_recv[q].astype(F32)).astype(BF16)
+
+    other_half(0)
     ones = jnp.ones((16, COLS), BF16)
     sum_in = dot_nt(ones, gp[...])[0:1]
     sum_out = dot_nt(ones, gl[...])[0:1]
@@ -292,68 +304,53 @@
     sm_c[pl.ds(c, 1)] = tile.reshape(1, 8, 128)
     smc_group = Group(sm_c.at[0])
     smc_group.send(sm_c.at[c], sm_c.at[c], sibling)
+    other_half(1)
+    own_half(0)
+    own_half(1)
 
     x_cols = pl.ds(pl.multiple_of(x * 128, 128), 128)
     u_rows = pl.ds(pl.multiple_of(u * 32, 32), 32)
 
-    def own_half(q):
-        rows = pl.ds(pl.multiple_of(c * 512 + q * 256, 256), 256)
-        own[q] = dot_nt(lat[rows, :], gp[...])
-
-    def merge(q):
-        sib_groups[q].arrived()
-        part[q] = (own[q] + sib_recv[q].astype(F32)).astype(BF16)
-
-    own_half(0)
-    own_half(1)
-    merge(0)
-    x0_group = Group(x0_recv)
+    wo_group.arrived()
+    second = wo_part[:, pl.ds(pl.multiple_of(c * 256, 256), 256)] + wo_recv[...].astype(F32)
+    smc_group.arrived()
+    sums = jnp.concatenate([sm_c[0] + sm_c[1], jnp.zeros((8, 128), F32)], axis=0).astype(BF16)
+    for j in range(4):
+        cols = pl.ds(128 * j, 128)
+        both = second[32 * j:32 * j + 32]
+        part0[256:288, cols] = both[:, 0:128].astype(BF16)
+        part0[288:320, cols] = both[:, 128:256].astype(BF16)
+        part0[320:336, cols] = sums
+    x0_recv[x, 320:336] = sums
+    part0[0:256, :] = merged(0)
+    x0_group = Group(x0_recv.at[pl.ds(0, 3)])
     for k in FAR4:
         cols = pl.ds(pl.multiple_of(x_at[k] * 128, 128), 128)
-        x0_group.send(part.at[0, :, cols], x0_recv.at[k - 1], to_x[k])
-    merge(1)
+        x0_group.send(part0.at[:, cols], x0_recv.at[x], to_x[k])
+    part1[...] = merged(1)
     u1_group = Group(u1_recv)
     for k in FAR8:
         rows = pl.ds(pl.multiple_of(u_at[k] * 32, 32), 32)
-        u1_group.send(part.at[1, rows], u1_recv.at[k - 1], to_u[k])
-    wo_group.arrived()
-    wo_rs[...] = (
-        wo_part[pl.ds(pl.multiple_of(c * 256, 256), 256), :] + wo_recv[...].astype(F32)).astype(BF16)
-    wox_group = Group(wox_recv)
-    for k in FAR4:
-        rows = pl.ds(pl.multiple_of(x_at[k] * 64, 64), 64)
-        wox_group.send(wo_rs.at[rows], wox_recv.at[k - 1], to_x[k])
-    smc_group.arrived()
-    sm_x[pl.ds(x, 1)] = (sm_c[0] + sm_c[1]).reshape(1, 8, 128)
-    smx_group = Group(sm_x.at[pl.ds(0, 3)])
-    for k in FAR4:
-        smx_group.send(sm_x.at[x], sm_x.at[x], to_x[k])
+        u1_group.send(part1.at[rows], u1_recv.at[k - 1], to_u[k])
 
     drain()
     x0_group.arrived()
-    total = part[0, :, x_cols].astype(F32)
-    for k in range(3):
-        total = total + x0_recv[k].astype(F32)
-    s0[...] = total.astype(BF16)
-    u0_group = Group(u0_recv)
+    total = part0[0:320, x_cols].astype(F32)
+    for k in range(1, 4):
+        total = total + x0_recv[x_at[k], 0:320].astype(F32)
+    sums = x0_recv[0, 320:336].astype(F32)
+    for k in range(1, 4):
+        sums = sums + x0_recv[k, 320:336].astype(F32)
+    for j in range(8):
+        at = 256 + 32 * (j % 2) + 8 * (j // 2)
+        s0[j] = jnp.concatenate(
+            [total[32 * j:32 * j + 32], total[at:at + 8], sums[0:8]], axis=0).astype(BF16)
+    u0_recv[pl.ds(u, 1)] = s0[pl.ds(u, 1)]
+    u0_group = Group(u0_recv.at[pl.ds(0, 7)])
     for k in FAR8:
-        rows = pl.ds(pl.multiple_of(u_at[k] * 32, 32), 32)
-        u0_group.send(s0.at[rows], u0_recv.at[k - 1], to_u[k])
-    wox_group.arrived()
-    total = wo_rs[pl.ds(pl.multiple_of(x * 64, 64), 64), :].astype(F32)
-    for k in range(3):
-        total = total + wox_recv[k].astype(F32)
-    smx_group.arrived()
-    small = sm_x[0] + sm_x[1] + sm_x[2] + sm_x[3]
-    for j in range(8):
-        wou_src[j, 0:8] = total[8 * j:8 * j + 8]
-        wou_src[j, 8:16] = small
-    wou_recv[pl.ds(u, 1)] = wou_src[pl.ds(u, 1)]
-    wou_group = Group(wou_recv.at[pl.ds(0, 7)])
-    for k in FAR8:
-        wou_group.send(wou_src.at[u_at[k]], wou_recv.at[u], to_u[k])
+        u0_group.send(s0.at[u_at[k]], u0_recv.at[u], to_u[k])
     u1_group.arrived()
-    total = part[1, u_rows, :].astype(F32)
+    total = part1[u_rows, :].astype(F32)
     for k in range(7):
         total = total + u1_recv[k].astype(F32)
     s1[...] = total.astype(BF16)
@@ -366,79 +363,50 @@
     total = s1[:, x_cols].astype(F32)
     for k in range(3):
         total = total + x1_recv[k].astype(F32)
-    v_recv[v, 1] = total.astype(BF16)
+    v_recv[v, UNIT:UNIT + 32] = total.astype(BF16)
     u0_group.arrived()
-    total = s0[u_rows, :].astype(F32)
-    for k in range(7):
+    total = u0_recv[0].astype(F32)
+    for k in range(1, 8):
         total = total + u0_recv[k].astype(F32)
-    v_recv[v, 0] = total.astype(BF16)
+    v_recv[v, 0:UNIT] = total.astype(BF16)
     v_group = Group(v_recv.at[pl.ds(0, 7)])
     for k in FAR8:
         v_group.send(v_recv.at[v], v_recv.at[v], to_v[k])
-    wou_group.arrived()
-    total = wou_recv[0]
-    for k in range(1, 8):
-        total = total + wou_recv[k]
-    wov_recv[pl.ds(v, 1)] = total.reshape(1, 16, 128)
-    wov_group = Group(wov_recv.at[pl.ds(0, 7)])
-    for k in FAR8:
-        wov_group.send(wov_recv.at[v], wov_recv.at[v], to_v[k])
-    drain()
-
-    base = c * 512
-
-    def block(q, rows_at, rows, cols):
-        return gw_ref.at[pl.ds(pl.multiple_of(base + q * 256 + rows_at, 32), rows), cols]
+    drain()
+
+    def block(rows_at, rows, cols):
+        return gw_ref.at[pl.ds(pl.multiple_of(c * 512 + rows_at, 32), rows), cols]
 
     v_group.arrived()
     total = v_recv[0].astype(F32)
     for k in range(1, 8):
         total = total + v_recv[k].astype(F32)
-    total = total.astype(BF16)
-    spot1 = block(1, u * 32, 32, x_cols)
-    spot1[...] = total[1]
-    spot0 = block(0, u * 32, 32, x_cols)
-    spot0[...] = total[0]
-    u0_group = Group(u0_recv)
+    gather[x, u] = total[0:UNIT].astype(BF16)
+    u0_group = Group(u0_recv.at[pl.ds(0, 7)])
     for k in FAR8:
-        u0_group.send(spot0, spot0, to_u[k])
+        u0_group.send(gather.at[x, u], gather.at[x, u], to_u[k])
+    spot = block(256 + u * 32, 32, x_cols)
+    spot[...] = total[UNIT:UNIT + 32].astype(BF16)
     x1_group = Group(x1_recv)
     for k in FAR4:
-        x1_group.send(spot1, spot1, to_x[k])
-    wov_group.arrived()
-    total = wov_recv[0]
-    for k in range(1, 8):
-        total = total + wov_recv[k]
-    spot = gwo.at[pl.ds(pl.multiple_of(c * 256 + x * 64 + u * 8, 8), 8)]
-    spot[...] = total[0:8]
-    wou_group = Group(loss_recv.at[pl.ds(0, 7)])
-    for k in FAR8:
-        wou_group.send(spot, spot, to_u[k])
+        x1_group.send(spot, spot, to_x[k])
     for i in range(4):
-        gbin_ref[:, 128 * i:128 * i + 128] = total[8 + i:9 + i]
-    gbo_ref[...] = total[12:13, 0:VARS]
+        gbin_ref[:, 128 * i:128 * i + 128] = total[40 + i:41 + i]
+    gbo_ref[...] = total[44:45, 0:VARS]
     drain()
 
     x1_group.arrived()
-    spot = block(1, u * 32, 32, pl.ds(0, 512))
-    u1_group, last = Group(u1_recv), Group(part)
+    spot = block(256 + u * 32, 32, pl.ds(0, 512))
+    u1_group, last1 = Group(u1_recv), Group(part1)
     for k in FAR8:
         u1_group.send(spot, spot, to_u[k])
-        last.send(spot, spot, to_u_other[k])
-    last.send(spot, spot, sibling)
+        last1.send(spot, spot, to_u_other[k])
+    last1.send(spot, spot, sibling)
     u0_group.arrived()
-    spot = block(0, 0, 256, x_cols)
-    x0_group = Group(x0_recv, apart=3)
-    x0_copies = [x0_group.send(spot, spot, to_x[k]) for k in FAR4]
-    last.send(spot, spot, sibling)
-    wou_group.arrived()
-    rows = pl.ds(pl.multiple_of(c * 256 + x * 64, 64), 64)
-    spot = gwo_low.at[rows]
-    spot[...] = gwo[rows].astype(BF16)
-    wox_group = Group(wox_recv, apart=3)
-    wox_copies = [wox_group.send(spot, spot, to_x[k]) for k in FAR4]
-    last_wo = Group(wo_recv)
-    last_wo.send(spot, spot, sibling)
+    x0_group = Group(gather.at[pl.ds(0, 3)], apart=3)
+    x0_copies = [x0_group.send(gather.at[x], gather.at[x], to_x[k]) for k in FAR4]
+    last0 = Group(gather)
+    last0.send(gather.at[x], gather_other.at[x], sibling)
 
     drain()
     loss_group.arrived()
@@ -448,20 +416,27 @@
 
     for k, copy in reversed(list(zip(FAR4, x0_copies))):
         copy.wait_recv()
-        cols = pl.ds(pl.multiple_of(x_at[4 - k] * 128, 128), 128)
-        spot = block(0, 0, 256, cols)
-        last.send(spot, spot, sibling)
-    for k, copy in reversed(list(zip(FAR4, wox_copies))):
-        copy.wait_recv()
-        spot = gwo_low.at[pl.ds(pl.multiple_of(c * 256 + x_at[4 - k] * 64, 64), 64)]
-        last_wo.send(spot, spot, sibling)
-    last_wo.arrived()
-    gwo_ref[...] = jnp.transpose(gwo_low[...].astype(F32))[0:VARS]
+        last0.send(gather.at[x_at[4 - k]], gather_other.at[x_at[4 - k]], sibling)
+
+    def place(source, core):
+        for i in range(4):
+            for j in range(8):
+                rows = pl.ds(pl.multiple_of(core * 512 + 32 * j, 32), 32)
+                gw_ref[rows, 128 * i:128 * i + 128] = source[i, j, 0:32]
+                first_row = 32 * i + 8 * (j // 2)
+                count = min(8, VARS - first_row)
+                if count > 0:
+                    cols = pl.ds(pl.multiple_of(core * 256 + 128 * (j % 2), 128), 128)
+                    gwo_ref[first_row:first_row + count, cols] = source[i, j, 32:48].astype(F32)[0:count]
+
+    place(gather, c)
     u1_group.arrived()
-    last.arrived()
-    drain()
-    drain()
-    assert len(groups) == N_SENDS and received[0] == N_RECEIVES
+    last1.arrived()
+    last0.arrived()
+    place(gather_other, 1 - c)
+    drain()
+    drain()
+    assert (len(groups), received[0]) == (N_SENDS, N_RECEIVES), (len(groups), received[0])
 
 
 def deliver(*refs):
@@ -502,8 +477,7 @@
         out_specs=(vmem,) * 5,
         scratch_shapes=[
             scratch(F32, 1, HID), scratch(BF16, VARS, HID), scratch(F32, 1, VARS),
-            scratch(F32, VARS, COLS), scratch(F32, 1, COLS), scratch(F32, HID, 128),
-            scratch(BF16, HID, 128),
+            scratch(F32, VARS, COLS), scratch(F32, 1, COLS),
             scratch(BF16, DIN, COLS), scratch(BF16, DIN, HID),
             scratch(F32, HID, 128), scratch(F32, HID, COLS), scratch(F32, HID, COLS),
             scratch(BF16, HID, COLS), scratch(BF16, HID, 128), scratch(BF16, 128, HID),
@@ -512,15 +486,15 @@
             scratch(BF16, 8, FOLD, 128), scratch(BF16, 8, FOLD, 128),
             scratch(F32, 8, 8, 128), scratch(BF16, 128, COLS), scratch(BF16, HID, COLS),
             scratch(BF16, 2, 256, HID), scratch(BF16, 2, 256, HID),
-            scratch(F32, 2, 256, HID), scratch(BF16, 2, 256, HID),
-            scratch(BF16, 3, 256, 128), scratch(BF16, 256, 128),
-            scratch(BF16, 7, 32, 128),
-            scratch(BF16, 7, 32, HID), scratch(BF16, 32, HID),
-            scratch(BF16, 3, 32, 128), scratch(BF16, 8, 2, 32, 128),
-            scratch(F32, HID, 128), scratch(BF16, 256, 128), scratch(BF16, 256, 128),
-            scratch(BF16, 256, 128), scratch(BF16, 3, 64, 128),
-            scratch(F32, 8, 16, 128), scratch(F32, 8, 16, 128), scratch(F32, 8, 16, 128),
-            scratch(F32, 2, 8, 128), scratch(F32, 4, 8, 128),
+            scratch(F32, 2, 256, HID),
+            scratch(F32, 128, HID), scratch(BF16, 128, 256), scratch(BF16, 128, 256),
+            scratch(F32, 2, 8, 128),
+            scratch(BF16, 336, HID), scratch(BF16, 4, 336, 128),
+            scratch(BF16, 8, UNIT, 128), scratch(BF16, 8, UNIT, 128),
+            scratch(BF16, 256, HID), scratch(BF16, 7, 32, HID),
+            scratch(BF16, 32, HID), scratch(BF16, 3, 32, 128),
+            scratch(BF16, 8, UNIT + 32, 128),
+            scratch(BF16, 4, 8, UNIT, 128), scratch(BF16, 4, 8, UNIT, 128),
             pltpu.SemaphoreType.DMA((9,)),
             pltpu.SemaphoreType.DMA((N_SENDS,)), pltpu.SemaphoreType.DMA((N_RECEIVES,)),
         ],

time: 56.6 us -> 57.4 us (1.014)
  Pallas kernels: 55.8 us -> 56.6 us
    pallas_call x1, Pallas kernels: 54.8 us -> 55.5 us  [per_device(): pl.pallas_call(lambda *refs: kernel(total_columns, *refs), out_shape=resu...]
where the time goes in v6:
time: 57.4 us; the launch traced here: 57.3 us
  Pallas kernels  56.6 us (99%)
  between operations  0.64 us (1%)
    pallas_call x1, Pallas kernels, per_device(): pl.pallas_call(lambda *refs: kernel(total_columns, *refs), out_shape=resu...  55.5 us

profile of v6, /device:TPU:1, one launch (start us, length us, event | category | flops | bytes accessed | tf_op | source)
XLA Modules:
  0.0 57.3 jit_solution(10012116306908698319)
XLA Ops:
  0.6 55.5 %energy_score_step.1 = (f32[1,512]{1,0:T(1,128)S(1)}, bf16[1024,512]{1,0:T(8,128)(2,1)S(1)}, f32[1,512]{1,0:T(1,128)S(1)}, f32[83,512]{1,0:T(8,128)S(1)}, f32[1,83]{1,0:T(1,128)S(1)}) custom-call(bf16[1,1024,512]{2,1,0:T(8,128)(2,1)} %refs_0_.1, bf16[1024,512]{1,0:T(8,128)(2,1)} %refs_1_.1, f32[1,512]{1,0:T(1,128)} %bitcast.10, bf16[83,512]{1,0:T(8,128)(2,1)} %bitcast.9, ...), custom_call_target="tpu_custom_call" | custom-call | flops 1073741824 | bytes 4194304 | tf_op jit(solution)/shard_map/energy_score_step/pallas_call | solution.py:473
  56.2 1.1 %deliver.1 = (f32[1,512]{1,0:T(1,128)}, bf16[1024,512]{1,0:T(8,128)(2,1)}, f32[1,512]{1,0:T(1,128)}, f32[83,512]{1,0:T(8,128)}, f32[1,83]{1,0:T(1,128)}) custom-call(f32[1,512]{1,0:T(1,128)S(1)} %get-tuple-element.15.refs_0_, bf16[1024,512]{1,0:T(8,128)(2,1)S(1)} %get-tuple-element.16.refs_1_, f32[1,512]{1,0:T(1,128)S(1)} %get-tuple-element.17.refs_2_, ...), custom_call_target="tpu_custom_call" | custom-call | tf_op jit(solution)/shard_map/deliver/pallas_call | solution.py:507

commit v7 on v6

--- a/solution.py
+++ b/solution.py
@@ -17,11 +17,13 @@
 DIN, HID, VARS = 1024, 512, 83
 COLS = 512
 FOLD = 48
-UNIT = 48
+ROWS0, ROWS1 = 128, 384
+CHUNK0, CHUNK1 = ROWS0 // 8, ROWS1 // 8
+UNIT = CHUNK0 + 16
 NX, NU = 4, 8
 FAR4 = (2, 1, 3)
 FAR8 = (4, 3, 5, 2, 6, 1, 7)
-N_SENDS, N_RECEIVES = 18, 20
+N_SENDS, N_RECEIVES = 18, 26
 
 
 def dot(a, b):
@@ -67,7 +69,6 @@
     to_u = [device(x, u_at[k] * on_y + y * c, z * on_y + u_at[k] * c) for k in range(8)]
     to_v = [device(x, y * on_y + v_at[k] * c, v_at[k] * on_y + z * c) for k in range(8)]
 
-    to_u_other = [(there_u[0] + 1 - 2 * c, there_u[1]) for there_u in to_u]
     sibling = (zlo * 2 + 1 - c, grid)
 
     def flip(bit, by):
@@ -137,11 +138,11 @@
     barrier = pltpu.get_barrier_semaphore()
     far, near = rels[:4], rels[4:]
     partners = (
-        [way[k] for k in (4, 3, 5) for way in (to_u, to_u_other, to_v)]
+        [way[k] for k in (4, 3, 5) for way in (to_u, to_v)]
         + [(there[rel], grid) for rel in far]
-        + [way[k] for k in (2, 6) for way in (to_u, to_u_other, to_v)] + [to_x[2]]
+        + [way[k] for k in (2, 6) for way in (to_u, to_v)] + [to_x[2]]
         + [(there[rel], grid) for rel in near]
-        + [way[k] for k in (1, 7) for way in (to_u, to_u_other, to_v)] + [to_x[1], to_x[3]]
+        + [way[k] for k in (1, 7) for way in (to_u, to_v)] + [to_x[1], to_x[3]]
     )
     for partner in partners:
         pl.semaphore_signal(barrier, inc=1, device_id=partner, device_id_type=MESH)
@@ -278,20 +279,22 @@
 
     lax.fori_loop(0, HID // 128, grad_hidden, 0)
 
-    sib_groups = [Group(sib_recv.at[q]) for q in range(2)]
+    half = (pl.ds(0, ROWS0), pl.ds(ROWS0, ROWS1))
+    sib_groups = [Group(sib_recv.at[half[q]]) for q in range(2)]
+
+    def rows_of(core, q):
+        return pl.ds(pl.multiple_of(core * 512 + q * ROWS0, 128), (ROWS0, ROWS1)[q])
 
     def other_half(q):
-        rows = pl.ds(pl.multiple_of((1 - c) * 512 + q * 256, 256), 256)
-        sib_send[q] = dot_nt(lat[rows, :], gp[...]).astype(BF16)
-        sib_groups[q].send(sib_send.at[q], sib_recv.at[q], sibling)
+        sib_send[half[q], :] = dot_nt(lat[rows_of(1 - c, q), :], gp[...]).astype(BF16)
+        sib_groups[q].send(sib_send.at[half[q]], sib_recv.at[half[q]], sibling)
 
     def own_half(q):
-        rows = pl.ds(pl.multiple_of(c * 512 + q * 256, 256), 256)
-        own[q] = dot_nt(lat[rows, :], gp[...])
+        own[half[q], :] = dot_nt(lat[rows_of(c, q), :], gp[...])
 
     def merged(q):
         sib_groups[q].arrived()
-        return (own[q] + sib_recv[q].astype(F32)).astype(BF16)
+        return (own[half[q], :] + sib_recv[half[q], :].astype(F32)).astype(BF16)
 
     other_half(0)
     ones = jnp.ones((16, COLS), BF16)
@@ -309,7 +312,8 @@
     own_half(1)
 
     x_cols = pl.ds(pl.multiple_of(x * 128, 128), 128)
-    u_rows = pl.ds(pl.multiple_of(u * 32, 32), 32)
+    u_rows = pl.ds(pl.multiple_of(u * CHUNK1, 16), CHUNK1)
+    last_rows = pl.ds(ROWS0 + 64, 16)
 
     wo_group.arrived()
     second = wo_part[:, pl.ds(pl.multiple_of(c * 256, 256), 256)] + wo_recv[...].astype(F32)
@@ -318,11 +322,11 @@
     for j in range(4):
         cols = pl.ds(128 * j, 128)
         both = second[32 * j:32 * j + 32]
-        part0[256:288, cols] = both[:, 0:128].astype(BF16)
-        part0[288:320, cols] = both[:, 128:256].astype(BF16)
-        part0[320:336, cols] = sums
-    x0_recv[x, 320:336] = sums
-    part0[0:256, :] = merged(0)
+        part0[ROWS0:ROWS0 + 32, cols] = both[:, 0:128].astype(BF16)
+        part0[ROWS0 + 32:ROWS0 + 64, cols] = both[:, 128:256].astype(BF16)
+        part0[last_rows, cols] = sums
+    x0_recv[x, last_rows] = sums
+    part0[0:ROWS0, :] = merged(0)
     x0_group = Group(x0_recv.at[pl.ds(0, 3)])
     for k in FAR4:
         cols = pl.ds(pl.multiple_of(x_at[k] * 128, 128), 128)
@@ -330,21 +334,21 @@
     part1[...] = merged(1)
     u1_group = Group(u1_recv)
     for k in FAR8:
-        rows = pl.ds(pl.multiple_of(u_at[k] * 32, 32), 32)
+        rows = pl.ds(pl.multiple_of(u_at[k] * CHUNK1, 16), CHUNK1)
         u1_group.send(part1.at[rows], u1_recv.at[k - 1], to_u[k])
 
     drain()
     x0_group.arrived()
-    total = part0[0:320, x_cols].astype(F32)
+    total = part0[0:ROWS0 + 64, x_cols].astype(F32)
     for k in range(1, 4):
-        total = total + x0_recv[x_at[k], 0:320].astype(F32)
-    sums = x0_recv[0, 320:336].astype(F32)
+        total = total + x0_recv[x_at[k], 0:ROWS0 + 64].astype(F32)
+    sums = x0_recv[0, last_rows].astype(F32)
     for k in range(1, 4):
-        sums = sums + x0_recv[k, 320:336].astype(F32)
+        sums = sums + x0_recv[k, last_rows].astype(F32)
     for j in range(8):
-        at = 256 + 32 * (j % 2) + 8 * (j // 2)
+        at = ROWS0 + 32 * (j % 2) + 8 * (j // 2)
         s0[j] = jnp.concatenate(
-            [total[32 * j:32 * j + 32], total[at:at + 8], sums[0:8]], axis=0).astype(BF16)
+            [total[CHUNK0 * j:CHUNK0 * (j + 1)], total[at:at + 8], sums[0:8]], axis=0).astype(BF16)
     u0_recv[pl.ds(u, 1)] = s0[pl.ds(u, 1)]
     u0_group = Group(u0_recv.at[pl.ds(0, 7)])
     for k in FAR8:
@@ -363,7 +367,7 @@
     total = s1[:, x_cols].astype(F32)
     for k in range(3):
         total = total + x1_recv[k].astype(F32)
-    v_recv[v, UNIT:UNIT + 32] = total.astype(BF16)
+    v_recv[v, UNIT:UNIT + CHUNK1] = total.astype(BF16)
     u0_group.arrived()
     total = u0_recv[0].astype(F32)
     for k in range(1, 8):
@@ -375,7 +379,7 @@
     drain()
 
     def block(rows_at, rows, cols):
-        return gw_ref.at[pl.ds(pl.multiple_of(c * 512 + rows_at, 32), rows), cols]
+        return gw_ref.at[pl.ds(pl.multiple_of(c * 512 + rows_at, 16), rows), cols]
 
     v_group.arrived()
     total = v_recv[0].astype(F32)
@@ -385,22 +389,21 @@
     u0_group = Group(u0_recv.at[pl.ds(0, 7)])
     for k in FAR8:
         u0_group.send(gather.at[x, u], gather.at[x, u], to_u[k])
-    spot = block(256 + u * 32, 32, x_cols)
-    spot[...] = total[UNIT:UNIT + 32].astype(BF16)
+    spot = block(ROWS0 + u * CHUNK1, CHUNK1, x_cols)
+    spot[...] = total[UNIT:UNIT + CHUNK1].astype(BF16)
     x1_group = Group(x1_recv)
     for k in FAR4:
         x1_group.send(spot, spot, to_x[k])
     for i in range(4):
-        gbin_ref[:, 128 * i:128 * i + 128] = total[40 + i:41 + i]
-    gbo_ref[...] = total[44:45, 0:VARS]
+        gbin_ref[:, 128 * i:128 * i + 128] = total[UNIT - 8 + i:UNIT - 7 + i]
+    gbo_ref[...] = total[UNIT - 4:UNIT - 3, 0:VARS]
     drain()
 
     x1_group.arrived()
-    spot = block(256 + u * 32, 32, pl.ds(0, 512))
-    u1_group, last1 = Group(u1_recv), Group(part1)
-    for k in FAR8:
-        u1_group.send(spot, spot, to_u[k])
-        last1.send(spot, spot, to_u_other[k])
+    spot = block(ROWS0 + u * CHUNK1, CHUNK1, pl.ds(0, 512))
+    u1_group = Group(u1_recv, apart=7)
+    u1_copies = [u1_group.send(spot, spot, to_u[k]) for k in FAR8]
+    last1 = Group(part1)
     last1.send(spot, spot, sibling)
     u0_group.arrived()
     x0_group = Group(gather.at[pl.ds(0, 3)], apart=3)
@@ -414,23 +417,28 @@
         loss_ref[:, 128 * t:128 * t + 128] = jnp.where(
             low_row, loss_recv[2 * t, 0:1, :], loss_recv[2 * t + 1, 0:1, :])
 
-    for k, copy in reversed(list(zip(FAR4, x0_copies))):
+    near_u = [(k, copy, False) for k, copy in zip(FAR8, u1_copies)][::-1]
+    near_x = [(k, copy, True) for k, copy in zip(FAR4, x0_copies)][::-1]
+    for k, copy, along_x in near_u[:4] + near_x[:2] + near_u[4:] + near_x[2:]:
         copy.wait_recv()
-        last0.send(gather.at[x_at[4 - k]], gather_other.at[x_at[4 - k]], sibling)
+        if along_x:
+            last0.send(gather.at[x_at[4 - k]], gather_other.at[x_at[4 - k]], sibling)
+        else:
+            spot = block(ROWS0 + u_at[8 - k] * CHUNK1, CHUNK1, pl.ds(0, 512))
+            last1.send(spot, spot, sibling)
 
     def place(source, core):
         for i in range(4):
             for j in range(8):
-                rows = pl.ds(pl.multiple_of(core * 512 + 32 * j, 32), 32)
-                gw_ref[rows, 128 * i:128 * i + 128] = source[i, j, 0:32]
+                rows = pl.ds(pl.multiple_of(core * 512 + CHUNK0 * j, 16), CHUNK0)
+                gw_ref[rows, 128 * i:128 * i + 128] = source[i, j, 0:CHUNK0]
                 first_row = 32 * i + 8 * (j // 2)
                 count = min(8, VARS - first_row)
                 if count > 0:
                     cols = pl.ds(pl.multiple_of(core * 256 + 128 * (j % 2), 128), 128)
-                    gwo_ref[first_row:first_row + count, cols] = source[i, j, 32:48].astype(F32)[0:count]
+                    gwo_ref[first_row:first_row + count, cols] = source[i, j, CHUNK0:UNIT].astype(F32)[0:count]
 
     place(gather, c)
-    u1_group.arrived()
     last1.arrived()
     last0.arrived()
     place(gather_other, 1 - c)
@@ -485,15 +493,15 @@
             scratch(BF16, 2, 2, 2, FOLD, 128), scratch(BF16, 8, FOLD, 128),
             scratch(BF16, 8, FOLD, 128), scratch(BF16, 8, FOLD, 128),
             scratch(F32, 8, 8, 128), scratch(BF16, 128, COLS), scratch(BF16, HID, COLS),
-            scratch(BF16, 2, 256, HID), scratch(BF16, 2, 256, HID),
-            scratch(F32, 2, 256, HID),
+            scratch(BF16, 512, HID), scratch(BF16, 512, HID),
+            scratch(F32, 512, HID),
             scratch(F32, 128, HID), scratch(BF16, 128, 256), scratch(BF16, 128, 256),
             scratch(F32, 2, 8, 128),
-            scratch(BF16, 336, HID), scratch(BF16, 4, 336, 128),
+            scratch(BF16, ROWS0 + 80, HID), scratch(BF16, 4, ROWS0 + 80, 128),
             scratch(BF16, 8, UNIT, 128), scratch(BF16, 8, UNIT, 128),
-            scratch(BF16, 256, HID), scratch(BF16, 7, 32, HID),
-            scratch(BF16, 32, HID), scratch(BF16, 3, 32, 128),
-            scratch(BF16, 8, UNIT + 32, 128),
+            scratch(BF16, ROWS1, HID), scratch(BF16, 7, CHUNK1, HID),
+            scratch(BF16, CHUNK1, HID), scratch(BF16, 3, CHUNK1, 128),
+            scratch(BF16, 8, UNIT + CHUNK1, 128),
             scratch(BF16, 4, 8, UNIT, 128), scratch(BF16, 4, 8, UNIT, 128),
             pltpu.SemaphoreType.DMA((9,)),
             pltpu.SemaphoreType.DMA((N_SENDS,)), pltpu.SemaphoreType.DMA((N_RECEIVES,)),

time: 57.4 us -> 58.9 us (1.026)
  Pallas kernels: 56.6 us -> 58.1 us
    pallas_call x1, Pallas kernels: 55.5 us -> 57 us  [per_device(): pl.pallas_call(lambda *refs: kernel(total_columns, *refs), out_shape=resu...]
where the time goes in v7:
time: 58.9 us; the launch traced here: 58.8 us
  Pallas kernels  58.1 us (99%)
  between operations  0.64 us (1%)
    pallas_call x1, Pallas kernels, per_device(): pl.pallas_call(lambda *refs: kernel(total_columns, *refs), out_shape=resu...  57 us

profile of v7, /device:TPU:1, one launch (start us, length us, event | category | flops | bytes accessed | tf_op | source)
XLA Modules:
  0.0 58.8 jit_solution(16801368222213288874)
XLA Ops:
  0.6 57.0 %energy_score_step.1 = (f32[1,512]{1,0:T(1,128)S(1)}, bf16[1024,512]{1,0:T(8,128)(2,1)S(1)}, f32[1,512]{1,0:T(1,128)S(1)}, f32[83,512]{1,0:T(8,128)S(1)}, f32[1,83]{1,0:T(1,128)S(1)}) custom-call(bf16[1,1024,512]{2,1,0:T(8,128)(2,1)} %refs_0_.1, bf16[1024,512]{1,0:T(8,128)(2,1)} %refs_1_.1, f32[1,512]{1,0:T(1,128)} %bitcast.10, bf16[83,512]{1,0:T(8,128)(2,1)} %bitcast.9, ...), custom_call_target="tpu_custom_call" | custom-call | flops 1073741824 | bytes 4194304 | tf_op jit(solution)/shard_map/energy_score_step/pallas_call | solution.py:481
  57.7 1.1 %deliver.1 = (f32[1,512]{1,0:T(1,128)}, bf16[1024,512]{1,0:T(8,128)(2,1)}, f32[1,512]{1,0:T(1,128)}, f32[83,512]{1,0:T(8,128)}, f32[1,83]{1,0:T(1,128)}) custom-call(f32[1,512]{1,0:T(1,128)S(1)} %get-tuple-element.15.refs_0_, bf16[1024,512]{1,0:T(8,128)(2,1)S(1)} %get-tuple-element.16.refs_1_, f32[1,512]{1,0:T(1,128)S(1)} %get-tuple-element.17.refs_2_, ...), custom_call_target="tpu_custom_call" | custom-call | tf_op jit(solution)/shard_map/deliver/pallas_call | solution.py:515

commit v8 on v5

--- a/solution.py
+++ b/solution.py
@@ -20,7 +20,7 @@
 NX, NU = 4, 8
 FAR4 = (2, 1, 3)
 FAR8 = (4, 3, 5, 2, 6, 1, 7)
-N_SENDS, N_RECEIVES = 24, 28
+N_SENDS, N_RECEIVES = 24, 34
 
 
 def dot(a, b):
@@ -248,9 +248,10 @@
             grads[n] = grads[n] + pull
     for m in range(8):
         g_send[m] = grads[m].astype(BF16)
-    g_group = Group(g_recv.at[pl.ds(0, 7)])
-    for rel in rels:
-        g_group.send(g_send.at[there[rel]], g_recv.at[member], (there[rel], grid))
+    g_group = Group(g_recv.at[pl.ds(0, 7)], apart=7)
+    g_copies = {
+        rel: g_group.send(g_send.at[there[rel]], g_recv.at[member], (there[rel], grid))
+        for rel in rels}
     g_recv[pl.ds(member, 1)] = g_send[pl.ds(member, 1)]
     loss = true_total * (1.0 / 8) - pair_total * (1.0 / 128)
     loss_recv[pl.ds(member, 1)] = jnp.broadcast_to(loss, (1, 8, 128))
@@ -259,19 +260,16 @@
         loss_group.send(loss_recv.at[member], loss_recv.at[member], (there[rel], grid))
 
     drain()
-    g_group.arrived()
-    for t in range(4):
+    for ra, rb in ((0, 0), (0, 1), (1, 0), (1, 1)):
+        for rel in rels:
+            if rel[:2] == (ra, rb):
+                g_copies[rel].wait_recv()
+        t = 2 * flip(a, ra) + flip(b, rb)
         left, right = g_recv[2 * t].astype(F32), g_recv[2 * t + 1].astype(F32)
-        cols = pl.ds(128 * t, 128)
+        cols = pl.ds(pl.multiple_of(128 * t, 128), 128)
         gl[0:FOLD, cols] = jnp.where(low_lane, left, swap(right)).astype(BF16)
         gl[FOLD:2 * FOLD, cols] = jnp.where(low_lane, swap(left), right).astype(BF16)
-
-    def grad_hidden(r, _):
-        rows = pl.ds(pl.multiple_of(r * 128, 128), 128)
-        gp[rows, :] = (dot(wop[rows, :], gl[...]) * dgelu[rows, :]).astype(BF16)
-        return 0
-
-    lax.fori_loop(0, HID // 128, grad_hidden, 0)
+        gp[:, cols] = (dot(wop[...], gl[:, cols]) * dgelu[:, cols]).astype(BF16)
 
     sib_groups = [Group(sib_recv.at[q]) for q in range(2)]
     for q in range(2):

time: 56.6 us -> 56.2 us (level)
  no operation moved by 1% of the time
where the time goes in v8:
time: 56.2 us; the launch traced here: 56.1 us
  Pallas kernels  55.5 us (99%)
  between operations  0.64 us (1%)
    pallas_call x1, Pallas kernels, per_device(): pl.pallas_call(lambda *refs: kernel(total_columns, *refs), out_shape=resu...  54.4 us

profile of v8, /device:TPU:1, one launch (start us, length us, event | category | flops | bytes accessed | tf_op | source)
XLA Modules:
  0.0 56.1 jit_solution(10609440511722937173)
XLA Ops:
  0.6 54.4 %energy_score_step.1 = (f32[1,512]{1,0:T(1,128)S(1)}, bf16[1024,512]{1,0:T(8,128)(2,1)S(1)}, f32[1,512]{1,0:T(1,128)S(1)}, f32[83,512]{1,0:T(8,128)S(1)}, f32[1,83]{1,0:T(1,128)S(1)}) custom-call(bf16[1,1024,512]{2,1,0:T(8,128)(2,1)} %refs_0_.1, bf16[1024,512]{1,0:T(8,128)(2,1)} %refs_1_.1, f32[1,512]{1,0:T(1,128)} %bitcast.10, bf16[83,512]{1,0:T(8,128)(2,1)} %bitcast.9, ...), custom_call_target="tpu_custom_call" | custom-call | flops 1073741824 | bytes 4194304 | tf_op jit(solution)/shard_map/energy_score_step/pallas_call | solution.py:496
  55.0 1.1 %deliver.1 = (f32[1,512]{1,0:T(1,128)}, bf16[1024,512]{1,0:T(8,128)(2,1)}, f32[1,512]{1,0:T(1,128)}, f32[83,512]{1,0:T(8,128)}, f32[1,83]{1,0:T(1,128)}) custom-call(f32[1,512]{1,0:T(1,128)S(1)} %get-tuple-element.15.refs_0_, bf16[1024,512]{1,0:T(8,128)(2,1)S(1)} %get-tuple-element.16.refs_1_, f32[1,512]{1,0:T(1,128)S(1)} %get-tuple-element.17.refs_2_, ...), custom_call_target="tpu_custom_call" | custom-call | tf_op jit(solution)/shard_map/deliver/pallas_call | solution.py:531

commit v9 on v8

--- a/solution.py
+++ b/solution.py
@@ -20,7 +20,7 @@
 NX, NU = 4, 8
 FAR4 = (2, 1, 3)
 FAR8 = (4, 3, 5, 2, 6, 1, 7)
-N_SENDS, N_RECEIVES = 24, 34
+N_SENDS, N_RECEIVES = 27, 49
 
 
 def dot(a, b):
@@ -43,7 +43,7 @@
     lat, win, bias, pre, dgelu, hidden, wop, wop_t, row, obs_pad,
     f_send, f_recv, g_send, g_recv, loss_recv, gl, gp,
     sib_send, sib_recv, own, part,
-    x0_recv, s0, u0_recv, u1_recv, s1, x1_recv, v_recv,
+    x0_recv, s0, u0_recv, u1_recv, w1_recv, s1, x1_recv, v_recv, w_recv,
     wo_part, wo_send, wo_recv, wo_rs, wox_recv, wou_src, wou_recv, wov_recv,
     sm_c, sm_x,
     local_sems, send_sems, recv_sems,
@@ -67,7 +67,6 @@
     to_u = [device(x, u_at[k] * on_y + y * c, z * on_y + u_at[k] * c) for k in range(8)]
     to_v = [device(x, y * on_y + v_at[k] * c, v_at[k] * on_y + z * c) for k in range(8)]
 
-    to_u_other = [(there_u[0] + 1 - 2 * c, there_u[1]) for there_u in to_u]
     sibling = (zlo * 2 + 1 - c, grid)
 
     def flip(bit, by):
@@ -137,11 +136,11 @@
     barrier = pltpu.get_barrier_semaphore()
     far, near = rels[:4], rels[4:]
     partners = (
-        [way[k] for k in (4, 3, 5) for way in (to_u, to_u_other, to_v)]
+        [way[k] for k in (4, 3, 5) for way in (to_u, to_v)]
         + [(there[rel], grid) for rel in far]
-        + [way[k] for k in (2, 6) for way in (to_u, to_u_other, to_v)] + [to_x[2]]
+        + [way[k] for k in (2, 6) for way in (to_u, to_v)] + [to_x[2]]
         + [(there[rel], grid) for rel in near]
-        + [way[k] for k in (1, 7) for way in (to_u, to_u_other, to_v)] + [to_x[1], to_x[3]]
+        + [way[k] for k in (1, 7) for way in (to_u, to_v)] + [to_x[1], to_x[3]]
     )
     for partner in partners:
         pl.semaphore_signal(barrier, inc=1, device_id=partner, device_id_type=MESH)
@@ -310,10 +309,12 @@
         cols = pl.ds(pl.multiple_of(x_at[k] * 128, 128), 128)
         x0_group.send(part.at[0, :, cols], x0_recv.at[k - 1], to_x[k])
     merge(1)
-    u1_group = Group(u1_recv)
-    for k in FAR8:
-        rows = pl.ds(pl.multiple_of(u_at[k] * 32, 32), 32)
+    u1_group, w1_group = Group(u1_recv), Group(w1_recv)
+    for k in FAR8:
+        rows = pl.ds(pl.multiple_of(u_at[k] * 16, 16), 16)
         u1_group.send(part.at[1, rows], u1_recv.at[k - 1], to_u[k])
+        rows = pl.ds(pl.multiple_of(128 + v_at[k] * 16, 16), 16)
+        w1_group.send(part.at[1, rows], w1_recv.at[k - 1], to_v[k])
     wo_group.arrived()
     wo_rs[...] = (
         wo_part[pl.ds(pl.multiple_of(c * 256, 256), 256), :] + wo_recv[...].astype(F32)).astype(BF16)
@@ -350,11 +351,12 @@
     wou_group = Group(wou_recv.at[pl.ds(0, 7)])
     for k in FAR8:
         wou_group.send(wou_src.at[u_at[k]], wou_recv.at[u], to_u[k])
-    u1_group.arrived()
-    total = part[1, u_rows, :].astype(F32)
-    for k in range(7):
-        total = total + u1_recv[k].astype(F32)
-    s1[...] = total.astype(BF16)
+    for group, received_1, at, place in ((u1_group, u1_recv, u * 16, 0), (w1_group, w1_recv, 128 + v * 16, 16)):
+        group.arrived()
+        total = part[1, pl.ds(pl.multiple_of(at, 16), 16), :].astype(F32)
+        for k in range(7):
+            total = total + received_1[k].astype(F32)
+        s1[place:place + 16, :] = total.astype(BF16)
     x1_group = Group(x1_recv)
     for k in FAR4:
         cols = pl.ds(pl.multiple_of(x_at[k] * 128, 128), 128)
@@ -364,15 +366,18 @@
     total = s1[:, x_cols].astype(F32)
     for k in range(3):
         total = total + x1_recv[k].astype(F32)
-    v_recv[v, 1] = total.astype(BF16)
+    total = total.astype(BF16)
+    v_recv[v, 32:48] = total[0:16]
+    w_recv[u] = total[16:32]
     u0_group.arrived()
     total = s0[u_rows, :].astype(F32)
     for k in range(7):
         total = total + u0_recv[k].astype(F32)
-    v_recv[v, 0] = total.astype(BF16)
-    v_group = Group(v_recv.at[pl.ds(0, 7)])
+    v_recv[v, 0:32] = total.astype(BF16)
+    v_group, w_group = Group(v_recv.at[pl.ds(0, 7)]), Group(w_recv.at[pl.ds(0, 7)])
     for k in FAR8:
         v_group.send(v_recv.at[v], v_recv.at[v], to_v[k])
+        w_group.send(w_recv.at[u], w_recv.at[u], to_u[k])
     wou_group.arrived()
     total = wou_recv[0]
     for k in range(1, 8):
@@ -386,23 +391,30 @@
     base = c * 512
 
     def block(q, rows_at, rows, cols):
-        return gw_ref.at[pl.ds(pl.multiple_of(base + q * 256 + rows_at, 32), rows), cols]
+        return gw_ref.at[pl.ds(pl.multiple_of(base + q * 256 + rows_at, 16), rows), cols]
 
     v_group.arrived()
     total = v_recv[0].astype(F32)
     for k in range(1, 8):
         total = total + v_recv[k].astype(F32)
     total = total.astype(BF16)
-    spot1 = block(1, u * 32, 32, x_cols)
-    spot1[...] = total[1]
     spot0 = block(0, u * 32, 32, x_cols)
-    spot0[...] = total[0]
+    spot0[...] = total[0:32]
     u0_group = Group(u0_recv)
     for k in FAR8:
         u0_group.send(spot0, spot0, to_u[k])
+    spot1 = block(1, u * 16, 16, x_cols)
+    spot1[...] = total[32:48]
+    w_group.arrived()
+    total = w_recv[0].astype(F32)
+    for k in range(1, 8):
+        total = total + w_recv[k].astype(F32)
+    spot2 = block(1, 128 + v * 16, 16, x_cols)
+    spot2[...] = total.astype(BF16)
     x1_group = Group(x1_recv)
     for k in FAR4:
         x1_group.send(spot1, spot1, to_x[k])
+        x1_group.send(spot2, spot2, to_x[k])
     wov_group.arrived()
     total = wov_recv[0]
     for k in range(1, 8):
@@ -418,12 +430,15 @@
     drain()
 
     x1_group.arrived()
-    spot = block(1, u * 32, 32, pl.ds(0, 512))
-    u1_group, last = Group(u1_recv), Group(part)
-    for k in FAR8:
-        u1_group.send(spot, spot, to_u[k])
-        last.send(spot, spot, to_u_other[k])
-    last.send(spot, spot, sibling)
+    spot1 = block(1, u * 16, 16, pl.ds(0, 512))
+    spot2 = block(1, 128 + v * 16, 16, pl.ds(0, 512))
+    u1_group, w1_group, last = Group(u1_recv, apart=7), Group(w1_recv, apart=7), Group(part)
+    u1_copies, w1_copies = [], []
+    for k in FAR8:
+        u1_copies.append(u1_group.send(spot1, spot1, to_u[k]))
+        w1_copies.append(w1_group.send(spot2, spot2, to_v[k]))
+    last.send(spot1, spot1, sibling)
+    last.send(spot2, spot2, sibling)
     u0_group.arrived()
     spot = block(0, 0, 256, x_cols)
     x0_group = Group(x0_recv, apart=3)
@@ -444,18 +459,31 @@
         loss_ref[:, 128 * t:128 * t + 128] = jnp.where(
             low_row, loss_recv[2 * t, 0:1, :], loss_recv[2 * t + 1, 0:1, :])
 
-    for k, copy in reversed(list(zip(FAR4, x0_copies))):
+    def forward(copy, spot):
         copy.wait_recv()
-        cols = pl.ds(pl.multiple_of(x_at[4 - k] * 128, 128), 128)
-        spot = block(0, 0, 256, cols)
         last.send(spot, spot, sibling)
+
+    def forward_rows(steps):
+        for i in steps:
+            k = FAR8[i]
+            forward(u1_copies[i], block(1, u_at[8 - k] * 16, 16, pl.ds(0, 512)))
+            forward(w1_copies[i], block(1, 128 + v_at[8 - k] * 16, 16, pl.ds(0, 512)))
+
+    def forward_columns(steps):
+        for i in steps:
+            cols = pl.ds(pl.multiple_of(x_at[4 - FAR4[i]] * 128, 128), 128)
+            forward(x0_copies[i], block(0, 0, 256, cols))
+
+    forward_rows((6, 5, 4, 3))
+    forward_columns((2, 1))
+    forward_rows((2, 1, 0))
+    forward_columns((0,))
     for k, copy in reversed(list(zip(FAR4, wox_copies))):
         copy.wait_recv()
         spot = gwo_low.at[pl.ds(pl.multiple_of(c * 256 + x_at[4 - k] * 64, 64), 64)]
         last_wo.send(spot, spot, sibling)
     last_wo.arrived()
     gwo_ref[...] = jnp.transpose(gwo_low[...].astype(F32))[0:VARS]
-    u1_group.arrived()
     last.arrived()
     drain()
     drain()
@@ -513,8 +541,8 @@
             scratch(F32, 2, 256, HID), scratch(BF16, 2, 256, HID),
             scratch(BF16, 3, 256, 128), scratch(BF16, 256, 128),
             scratch(BF16, 7, 32, 128),
-            scratch(BF16, 7, 32, HID), scratch(BF16, 32, HID),
-            scratch(BF16, 3, 32, 128), scratch(BF16, 8, 2, 32, 128),
+            scratch(BF16, 7, 16, HID), scratch(BF16, 7, 16, HID), scratch(BF16, 32, HID),
+            scratch(BF16, 3, 32, 128), scratch(BF16, 8, 48, 128), scratch(BF16, 8, 16, 128),
             scratch(F32, HID, 128), scratch(BF16, 256, 128), scratch(BF16, 256, 128),
             scratch(BF16, 256, 128), scratch(BF16, 3, 64, 128),
             scratch(F32, 8, 16, 128), scratch(F32, 8, 16, 128), scratch(F32, 8, 16, 128),

time: 56.2 us -> 56.2 us (level)
  no operation moved by 1% of the time
where the time goes in v9:
time: 56.2 us; the launch traced here: 56 us
  Pallas kernels  55.4 us (99%)
  between operations  0.64 us (1%)
    pallas_call x1, Pallas kernels, per_device(): pl.pallas_call(lambda *refs: kernel(total_columns, *refs), out_shape=resu...  54.3 us

profile of v9, /device:TPU:1, one launch (start us, length us, event | category | flops | bytes accessed | tf_op | source)
XLA Modules:
  0.0 56.0 jit_solution(18198108317182417813)
XLA Ops:
  0.6 54.3 %energy_score_step.1 = (f32[1,512]{1,0:T(1,128)S(1)}, bf16[1024,512]{1,0:T(8,128)(2,1)S(1)}, f32[1,512]{1,0:T(1,128)S(1)}, f32[83,512]{1,0:T(8,128)S(1)}, f32[1,83]{1,0:T(1,128)S(1)}) custom-call(bf16[1,1024,512]{2,1,0:T(8,128)(2,1)} %refs_0_.1, bf16[1024,512]{1,0:T(8,128)(2,1)} %refs_1_.1, f32[1,512]{1,0:T(1,128)} %bitcast.10, bf16[83,512]{1,0:T(8,128)(2,1)} %bitcast.9, ...), custom_call_target="tpu_custom_call" | custom-call | flops 1073741824 | bytes 4194304 | tf_op jit(solution)/shard_map/energy_score_step/pallas_call | solution.py:524
  55.0 1.1 %deliver.1 = (f32[1,512]{1,0:T(1,128)}, bf16[1024,512]{1,0:T(8,128)(2,1)}, f32[1,512]{1,0:T(1,128)}, f32[83,512]{1,0:T(8,128)}, f32[1,83]{1,0:T(1,128)}) custom-call(f32[1,512]{1,0:T(1,128)S(1)} %get-tuple-element.15.refs_0_, bf16[1024,512]{1,0:T(8,128)(2,1)S(1)} %get-tuple-element.16.refs_1_, f32[1,512]{1,0:T(1,128)S(1)} %get-tuple-element.17.refs_2_, ...), custom_call_target="tpu_custom_call" | custom-call | tf_op jit(solution)/shard_map/deliver/pallas_call | solution.py:559

commit v10 on v9

--- a/solution.py
+++ b/solution.py
@@ -37,9 +37,9 @@
 
 def kernel(
     total_columns,
-    lat_hbm, win_hbm, bin_hbm, wo_hbm, bo_hbm, obs_hbm, area_hbm,
+    lat_hbm, win_hbm, bin_hbm, wo_ref, bo_hbm, obs_hbm, area_hbm,
     loss_ref, gw_ref, gbin_ref, gwo_ref, gbo_ref,
-    bin_ref, wo_ref, bo_ref, obs_ref, area_ref, gwo, gwo_low,
+    bin_ref, bo_ref, obs_ref, area_ref, gwo, gwo_low,
     lat, win, bias, pre, dgelu, hidden, wop, wop_t, row, obs_pad,
     f_send, f_recv, g_send, g_recv, loss_recv, gl, gp,
     sib_send, sib_recv, own, part,
@@ -127,10 +127,9 @@
     load_small = [
         pltpu.make_async_copy(src, dst, local_sems.at[4 + i])
         for i, (src, dst) in enumerate((
-            (bin_hbm, bin_ref), (wo_hbm, wo_ref), (bo_hbm, bo_ref),
-            (obs_hbm, obs_ref), (area_hbm, area_ref)))
+            (bin_hbm, bin_ref), (bo_hbm, bo_ref), (obs_hbm, obs_ref), (area_hbm, area_ref)))
     ]
-    for copy in load_w + load_l[:1] + load_small[:3]:
+    for copy in load_w + load_l[:1] + load_small[:2]:
         copy.start()
 
     barrier = pltpu.get_barrier_semaphore()
@@ -144,12 +143,12 @@
     )
     for partner in partners:
         pl.semaphore_signal(barrier, inc=1, device_id=partner, device_id_type=MESH)
-    for copy in load_l[1:] + load_small[3:]:
+    for copy in load_l[1:] + load_small[2:]:
         copy.start()
 
     wop_t[...] = jnp.zeros_like(wop_t)
     row[...] = jnp.zeros_like(row)
-    for copy in load_small[:3]:
+    for copy in load_small[:2]:
         copy.wait()
     for i in range(4):
         bias[pl.ds(128 * i, 128), :] = jnp.transpose(
@@ -208,7 +207,7 @@
 
     lax.fori_loop(0, HID // 128, derive, 0)
     wop[...] = jnp.transpose(wop_t[...])
-    for copy in load_small[3:]:
+    for copy in load_small[2:]:
         copy.wait()
     obs_pad[...] = jnp.zeros_like(obs_pad)
     own_cols = pl.ds(pl.multiple_of(zlo * 128, 128), 128)
@@ -524,10 +523,10 @@
     made = pl.pallas_call(
         lambda *refs: kernel(total_columns, *refs),
         out_shape=results,
-        in_specs=[hbm] * 7,
+        in_specs=[hbm] * 3 + [vmem] + [hbm] * 3,
         out_specs=(vmem,) * 5,
         scratch_shapes=[
-            scratch(F32, 1, HID), scratch(BF16, VARS, HID), scratch(F32, 1, VARS),
+            scratch(F32, 1, HID), scratch(F32, 1, VARS),
             scratch(F32, VARS, COLS), scratch(F32, 1, COLS), scratch(F32, HID, 128),
             scratch(BF16, HID, 128),
             scratch(BF16, DIN, COLS), scratch(BF16, DIN, HID),
@@ -547,7 +546,7 @@
             scratch(BF16, 256, 128), scratch(BF16, 3, 64, 128),
             scratch(F32, 8, 16, 128), scratch(F32, 8, 16, 128), scratch(F32, 8, 16, 128),
             scratch(F32, 2, 8, 128), scratch(F32, 4, 8, 128),
-            pltpu.SemaphoreType.DMA((9,)),
+            pltpu.SemaphoreType.DMA((8,)),
             pltpu.SemaphoreType.DMA((N_SENDS,)), pltpu.SemaphoreType.DMA((N_RECEIVES,)),
         ],
         compiler_params=pltpu.CompilerParams(
@@ -555,7 +554,9 @@
         cost_estimate=pl.CostEstimate(
             flops=4 * DIN * HID * COLS, bytes_accessed=4 * 2**20, transcendentals=2 * HID * COLS),
         name="energy_score_step",
-    )(*[pltpu.with_memory_space_constraint(operand, pltpu.HBM) for operand in operands])
+    )(*[
+        operand if i == 3 else pltpu.with_memory_space_constraint(operand, pltpu.HBM)
+        for i, operand in enumerate(operands)])
     loss, grad_w_in, grad_b_in, grad_w_out, grad_b_out = pl.pallas_call(
         deliver,
         out_shape=results,

time: 56.2 us -> 57 us (1.014)
  local copies, waits for them, and re-layouts: 0 us -> 0.88 us
    unnamed x0 -> x2, local copies, waits for them, and re-layouts: none -> 0.88 us
where the time goes in v10:
time: 57 us; the launch traced here: 56.9 us
  Pallas kernels  55.3 us (97%)
  local copies, waits for them, and re-layouts  0.88 us (2%)
  between operations  0.65 us (1%)
    pallas_call x1, Pallas kernels, per_device(): pl.pallas_call(lambda *refs: kernel(total_columns, *refs), out_shape=resu...  54.2 us

profile of v10, /device:TPU:1, one launch (start us, length us, event | category | flops | bytes accessed | tf_op | source)
XLA Modules:
  0.0 56.9 jit_solution(17383359910108936735)
XLA Ops:
  0.6 0.0 copy-start
  0.6 0.9 %copy-done = bf16[512,83]{0,1:T(8,128)(2,1)S(1)} copy-done((bf16[512,83]{0,1:T(8,128)(2,1)S(1)}, bf16[512,83]{0,1:T(8,128)(2,1)}, u32[]{:S(2)}) %copy-start) | copy-done | bytes 85016
  1.5 54.2 %energy_score_step.1 = (f32[1,512]{1,0:T(1,128)S(1)}, bf16[1024,512]{1,0:T(8,128)(2,1)S(1)}, f32[1,512]{1,0:T(1,128)S(1)}, f32[83,512]{1,0:T(8,128)S(1)}, f32[1,83]{1,0:T(1,128)S(1)}) custom-call(bf16[1,1024,512]{2,1,0:T(8,128)(2,1)} %refs_0_.1, bf16[1024,512]{1,0:T(8,128)(2,1)} %refs_1_.1, f32[1,512]{1,0:T(1,128)} %bitcast.10, bf16[83,512]{1,0:T(8,128)(2,1)S(1)} %bitcast.8, ...), custom_call_target="tpu_custom_call" | custom-call | flops 1073741824 | bytes 4194304 | tf_op jit(solution)/shard_map/energy_score_step/pallas_call | solution.py:523
  55.8 1.1 %deliver.1 = (f32[1,512]{1,0:T(1,128)}, bf16[1024,512]{1,0:T(8,128)(2,1)}, f32[1,512]{1,0:T(1,128)}, f32[83,512]{1,0:T(8,128)}, f32[1,83]{1,0:T(1,128)}) custom-call(f32[1,512]{1,0:T(1,128)S(1)} %get-tuple-element.15.refs_0_, bf16[1024,512]{1,0:T(8,128)(2,1)S(1)} %get-tuple-element.16.refs_1_, f32[1,512]{1,0:T(1,128)S(1)} %get-tuple-element.17.refs_2_, ...), custom_call_target="tpu_custom_call" | custom-call | tf_op jit(solution)/shard_map/deliver/pallas_call | solution.py:560
Async XLA Ops:
  0.6 0.9 %copy-start = (bf16[512,83]{0,1:T(8,128)(2,1)S(1)}, bf16[512,83]{0,1:T(8,128)(2,1)}, u32[]{:S(2)}) copy-start(bf16[512,83]{0,1:T(8,128)(2,1)} %param.10) | copy-start | bytes 254980

commit v11 on v10

--- a/solution.py
+++ b/solution.py
@@ -37,10 +37,10 @@
 
 def kernel(
     total_columns,
-    lat_hbm, win_hbm, bin_hbm, wo_ref, bo_hbm, obs_hbm, area_hbm,
+    lat_hbm, win_hbm, bin_hbm, wop_t, bo_hbm, obs_hbm, area_hbm,
     loss_ref, gw_ref, gbin_ref, gwo_ref, gbo_ref,
     bin_ref, bo_ref, obs_ref, area_ref, gwo, gwo_low,
-    lat, win, bias, pre, dgelu, hidden, wop, wop_t, row, obs_pad,
+    lat, win, bias, pre, dgelu, hidden, wop, row, obs_pad,
     f_send, f_recv, g_send, g_recv, loss_recv, gl, gp,
     sib_send, sib_recv, own, part,
     x0_recv, s0, u0_recv, u1_recv, w1_recv, s1, x1_recv, v_recv, w_recv,
@@ -146,14 +146,12 @@
     for copy in load_l[1:] + load_small[2:]:
         copy.start()
 
-    wop_t[...] = jnp.zeros_like(wop_t)
     row[...] = jnp.zeros_like(row)
     for copy in load_small[:2]:
         copy.wait()
     for i in range(4):
         bias[pl.ds(128 * i, 128), :] = jnp.transpose(
             jnp.broadcast_to(bin_ref[:, pl.ds(128 * i, 128)], (128, 128)))
-    wop_t[0:VARS, :] = wo_ref[...]
     row[:, 0:VARS] = bo_ref[...]
     bias_out = jnp.transpose(jnp.broadcast_to(row[...], (128, 128)))[0:2 * FOLD]
     lane = lax.broadcasted_iota(jnp.int32, (FOLD, 128), 1)
@@ -517,7 +515,7 @@
         jax.ShapeDtypeStruct((1, VARS), F32),
     )
     operands = (
-        latent, w_in, b_in.reshape(1, HID), output_weight.T, output_bias.reshape(1, VARS),
+        latent, w_in, b_in.reshape(1, HID), jnp.pad(output_weight.T, ((0, 128 - VARS), (0, 0))), output_bias.reshape(1, VARS),
         observed_field, area.reshape(1, COLS),
     )
     made = pl.pallas_call(
@@ -531,7 +529,7 @@
             scratch(BF16, HID, 128),
             scratch(BF16, DIN, COLS), scratch(BF16, DIN, HID),
             scratch(F32, HID, 128), scratch(F32, HID, COLS), scratch(F32, HID, COLS),
-            scratch(BF16, HID, COLS), scratch(BF16, HID, 128), scratch(BF16, 128, HID),
+            scratch(BF16, HID, COLS), scratch(BF16, HID, 128),
             scratch(F32, 1, 128), scratch(F32, 2 * FOLD, 128),
             scratch(BF16, 2, 2, 2, FOLD, 128), scratch(BF16, 8, FOLD, 128),
             scratch(BF16, 8, FOLD, 128), scratch(BF16, 8, FOLD, 128),

time: 57 us -> 57.3 us (level)
    pad x0 -> x1, local copies, waits for them, and re-layouts: none -> 0.9 us  [per_device(): jnp.pad(output_weight.T, ((0, 128 - VARS), (0, 0)))]
    unnamed x2 -> x0, local copies, waits for them, and re-layouts: 0.88 us -> none
where the time goes in v11:
time: 57.3 us; the launch traced here: 57.1 us
  Pallas kernels  55.5 us (97%)
  local copies, waits for them, and re-layouts  0.9 us (2%)
  between operations  0.64 us (1%)
    pallas_call x1, Pallas kernels, per_device(): pl.pallas_call(lambda *refs: kernel(total_columns, *refs), out_shape=resu...  54.5 us

profile of v11, /device:TPU:1, one launch (start us, length us, event | category | flops | bytes accessed | tf_op | source)
XLA Modules:
  0.0 57.1 jit_solution(9916244469028184049)
XLA Ops:
  0.6 0.9 %pad.4.refs_3_ = bf16[128,512]{1,0:T(8,128)(2,1)S(1)} pad(bf16[83,512]{1,0:T(8,128)(2,1)} %bitcast.8, bf16[]{:T(256)} %constant.2.clone.1), padding=0_45x0_0 | pad | bytes 216066 | tf_op jit(solution)/shard_map/jit(_pad)/pad | solution.py:518
  1.5 54.5 %energy_score_step.1 = (f32[1,512]{1,0:T(1,128)S(1)}, bf16[1024,512]{1,0:T(8,128)(2,1)S(1)}, f32[1,512]{1,0:T(1,128)S(1)}, f32[83,512]{1,0:T(8,128)S(1)}, f32[1,83]{1,0:T(1,128)S(1)}) custom-call(bf16[1,1024,512]{2,1,0:T(8,128)(2,1)} %refs_0_.1, bf16[1024,512]{1,0:T(8,128)(2,1)} %refs_1_.1, f32[1,512]{1,0:T(1,128)} %bitcast.10, ...), custom_call_target="tpu_custom_call" | custom-call | flops 1073741824 | bytes 4194304 | tf_op jit(solution)/shard_map/energy_score_step/pallas_call | solution.py:521
  56.0 1.1 %deliver.1 = (f32[1,512]{1,0:T(1,128)}, bf16[1024,512]{1,0:T(8,128)(2,1)}, f32[1,512]{1,0:T(1,128)}, f32[83,512]{1,0:T(8,128)}, f32[1,83]{1,0:T(1,128)}) custom-call(f32[1,512]{1,0:T(1,128)S(1)} %get-tuple-element.15.refs_0_, bf16[1024,512]{1,0:T(8,128)(2,1)S(1)} %get-tuple-element.16.refs_1_, f32[1,512]{1,0:T(1,128)S(1)} %get-tuple-element.17.refs_2_, ...), custom_call_target="tpu_custom_call" | custom-call | tf_op jit(solution)/shard_map/deliver/pallas_call | solution.py:558
